TPU v7x, 512 devices: a whole 4x4x16 slice. The times are simulated.
512 devices in a mesh: patch: 128 (over x, z, core), slab: 4 (over y).
Axes of the slice: x: 4, y: 4, z: 16, core: 2. Of those that a mesh axis runs over, the one named last changes fastest.
Arguments:
- coarse_disp: float32 [2, 8, 4096, 128], P(None, 'slab', 'patch'), may hold values from -6 to 6
- coarse_vel: float32 [2, 8, 4096, 128], P(None, 'slab', 'patch'), may hold values from -6 to 6
- coarse_acc: float32 [2, 8, 4096, 128], P(None, 'slab', 'patch'), may hold values from -6 to 6
- horizon: int32 [8, 4096, 128], P('slab', 'patch'), may hold values from 2 to 6
- crack_flag: int32 [8, 4096, 128], P('slab', 'patch'), may hold values 0 or 1
- fine_disp: float32 [49152, 2, 256], P(('patch', 'slab')), may hold values from -6 to 6
- fine_vel: float32 [49152, 2, 256], P(('patch', 'slab')), may hold values from -6 to 6
- fine_acc: float32 [49152, 2, 256], P(('patch', 'slab')), may hold values from -6 to 6
- fine_owner: int32 [49152, 1], P(('patch', 'slab')), may hold values from 0 to 127; in each aligned block of 96 rows (0 to 95, 96 to 191, ...) at most 2 rows name the same one
- fine_anchor: int32 [49152], P(('patch', 'slab')), may hold values from 0 to 63
Outputs:
- coarse_accel: float32 [2, 8, 4096, 128], P(None, 'slab', 'patch')
- coarse_velocity: float32 [2, 8, 4096, 128], P(None, 'slab', 'patch')
- fine_accel: float32 [49152, 2, 256], P(('patch', 'slab'))
- fine_velocity: float32 [49152, 2, 256], P(('patch', 'slab'))
Inputs may be any that keep to these rules, and one draw needn't show every extreme that they name: `fine_owner`: among the 96 fine blocks of one device no patch is named by more than 2 blocks, a bound that some block reaches.
All inputs are finite; a program needn't handle non-finite values. No bound on the sum of `crack_flag` on one device may be relied on, other than what follows from the above.
Results may differ from a plain program's by a relative error of at most 0.0003.
Values sent between devices are 32-bit elements; how exact they have to be, the bound alone decides.
No kernel may reach another device: no remote copies, remote signals or barrier semaphores. Data moves between devices by JAX's collectives and lax.ppermute only.
A program may use at most 128 MiB of HBM per device.

v0:
```python
import jax
import jax.numpy as jnp
from jax import lax
from jax.sharding import PartitionSpec as P

RADIUS = 6


STEP = 0.5


def with_halo(block, sides, width):
    for axis, dim in sides:
        count = lax.axis_size(axis)
        forward = [(i, i + 1) for i in range(count - 1)]
        backward = [(target, source) for source, target in forward]
        low = lax.ppermute(
            lax.slice_in_dim(block, block.shape[dim] - width, None, axis=dim), axis, forward
        )
        high = lax.ppermute(lax.slice_in_dim(block, 0, width, axis=dim), axis, backward)
        block = jnp.concatenate([low, block, high], axis=dim)
    return block


def bond_offsets(radius):
    listing = []
    for along_x in range(-radius, radius + 1):
        for along_y in range(-radius, radius + 1):
            square = along_x * along_x + along_y * along_y
            if 0 < square <= radius * radius:
                listing.append((along_x, along_y, square))
    return listing


def shift_cells(values, along_y):
    if along_y == 0:
        return values
    width = values.shape[-1]
    if along_y > 0:
        filler = jnp.zeros(values.shape[:-1] + (along_y,), values.dtype)
        return jnp.concatenate([values[..., along_y:], filler], axis=-1)
    filler = jnp.zeros(values.shape[:-1] + (-along_y,), values.dtype)
    return jnp.concatenate([filler, values[..., : width + along_y]], axis=-1)


def plane_force(widened, inner_x, radius):
    centre = widened[:, :, radius : radius + inner_x, :]
    centre_present = (centre[2] > 0.0).astype(jnp.float32)
    centre_guard = jnp.where(centre[2] > 0.0, centre[2], 1.0)
    own_modulus = centre_present * 2.0 / (centre_guard * centre_guard)
    own_reach = centre[2] * centre[2]
    moved = {}
    for along_y in range(-radius, radius + 1):
        shifted = shift_cells(widened, along_y)
        present = (shifted[2] > 0.0).astype(jnp.float32)
        guarded = jnp.where(shifted[2] > 0.0, shifted[2], 1.0)
        modulus = present * 2.0 / (guarded * guarded)
        moved[along_y] = (shifted, present, modulus)
    force_x = jnp.zeros_like(centre[0])
    force_y = jnp.zeros_like(centre[0])
    for along_x, along_y, square in bond_offsets(radius):
        start_x = radius + along_x
        shifted, present, modulus = moved[along_y]
        beside_field = shifted[:, :, start_x : start_x + inner_x, :]
        beside_modulus = modulus[:, start_x : start_x + inner_x, :]
        beside_present = present[:, start_x : start_x + inner_x, :]
        own_inside = (own_reach >= square).astype(jnp.float32)
        beside_inside = (beside_field[2] * beside_field[2] >= square).astype(jnp.float32)
        weight = (own_modulus * own_inside * beside_present + beside_modulus * beside_inside) * (
            1.0 - centre[3] * beside_field[3]
        )
        stretch = along_x * (beside_field[0] - centre[0]) + along_y * (beside_field[1] - centre[1])
        bond_term = weight * stretch * (1.0 / float(square) ** 1.5)
        force_x = force_x + bond_term * along_x
        force_y = force_y + bond_term * along_y
    return (force_x, force_y)


def layer_force(layers, inner_z):
    present = (layers[2] > 0.0).astype(jnp.float32)
    guarded = jnp.where(layers[2] > 0.0, layers[2], 1.0)
    modulus = present * 2.0 / (guarded * guarded)
    own_part = layers[:, 1 : inner_z + 1]
    own_modulus = modulus[1 : inner_z + 1]
    total_x = jnp.zeros_like(own_part[0])
    total_y = jnp.zeros_like(own_part[0])
    for offset_z in (0, 2):
        beside_part = layers[:, offset_z : offset_z + inner_z]
        factor = present[offset_z : offset_z + inner_z] * (
            own_modulus + modulus[offset_z : offset_z + inner_z]
        )
        total_x = total_x + factor * (beside_part[0] - own_part[0])
        total_y = total_y + factor * (beside_part[1] - own_part[1])
    return (total_x, total_y)


def refine_row(coarse_rows):
    following = jnp.concatenate([coarse_rows[..., 1:], coarse_rows[..., -1:]], axis=-1)
    middle = 0.5 * (coarse_rows + following)
    joined = jnp.stack([coarse_rows, middle], axis=-1)
    return joined.reshape(coarse_rows.shape[:-1] + (2 * coarse_rows.shape[-1],))


def restrict_row(values):
    even_part = values[..., 0::2]
    odd_part = values[..., 1::2]
    shifted = jnp.concatenate([jnp.zeros_like(odd_part[..., :1]), odd_part[..., :-1]], axis=-1)
    ending = jnp.concatenate([jnp.zeros_like(odd_part[..., :-1]), odd_part[..., -1:]], axis=-1)
    return even_part + 0.5 * odd_part + 0.5 * (shifted + ending)


def chain_force(points):
    differ = points[..., 1:] - points[..., :-1]
    zero_col = jnp.zeros_like(points[..., :1])
    return jnp.concatenate([differ, zero_col], axis=-1) - jnp.concatenate(
        [zero_col, differ], axis=-1
    )


def body(
    coarse_disp,
    coarse_vel,
    coarse_acc,
    horizon,
    crack_flag,
    fine_disp,
    fine_vel,
    fine_acc,
    fine_owner,
    fine_anchor,
):
    half_square = 0.5 * STEP * STEP
    coarse_new = coarse_disp + STEP * coarse_vel + half_square * coarse_acc
    fine_new = fine_disp + STEP * fine_vel + half_square * fine_acc
    layer_count, inner_x, inner_y = (
        coarse_disp.shape[1],
        coarse_disp.shape[2],
        coarse_disp.shape[3],
    )
    fields = jnp.stack(
        [coarse_new[0], coarse_new[1], horizon.astype(jnp.float32), crack_flag.astype(jnp.float32)]
    )
    widened = with_halo(fields, (("patch", 2),), RADIUS)
    force_x, force_y = plane_force(widened, inner_x, RADIUS)
    layers = with_halo(fields[:3], (("slab", 1),), 1)
    layer_x, layer_y = layer_force(layers, layer_count)
    bond = jnp.stack([force_x + layer_x, force_y + layer_y])
    patches = lax.axis_size("patch")
    blocks = fine_disp.shape[0]
    fine_y = fine_disp.shape[2]
    capacity = 2 * ((blocks + patches - 1) // patches)
    slot_count = patches * capacity
    owner_patch = fine_owner[:, 0]
    choose = (owner_patch[:, None] == jnp.arange(patches, dtype=jnp.int32)[None, :]).astype(
        jnp.int32
    )
    before = jnp.cumsum(choose, axis=0) - choose
    slot_rank = jnp.sum(before * choose, axis=1)
    target = owner_patch * capacity + slot_rank
    flat_grid = coarse_new.reshape(2, layer_count * inner_x, inner_y)
    send_anchor = jnp.full((slot_count,), -1, jnp.int32).at[target].set(fine_anchor)
    send_disp = jnp.zeros((slot_count, 2, fine_y), jnp.float32).at[target].set(fine_new)
    got_disp, got_anchor = (
        lax.all_to_all(
            send_disp.reshape(patches, capacity, 2, fine_y),
            "patch",
            split_axis=0,
            concat_axis=0,
            tiled=True,
        ),
        lax.all_to_all(
            send_anchor.reshape(patches, capacity), "patch", split_axis=0, concat_axis=0, tiled=True
        ),
    )
    got_disp = got_disp.reshape(slot_count, 2, fine_y)
    got_anchor = got_anchor.reshape(slot_count)
    live_slot = got_anchor >= 0
    picked = jnp.where(live_slot, got_anchor, 0)
    taken = jnp.transpose(flat_grid[:, picked, :], (1, 0, 2))
    answer = jnp.where(live_slot[:, None, None], refine_row(taken) - got_disp, 0.0)
    reaction_slots = jnp.transpose(-restrict_row(answer), (1, 0, 2))
    reaction_sum = jnp.zeros_like(flat_grid).at[:, picked, :].add(reaction_slots)
    returned = lax.all_to_all(
        answer.reshape(patches, capacity, 2, fine_y),
        "patch",
        split_axis=0,
        concat_axis=0,
        tiled=True,
    )
    coupling = returned.reshape(slot_count, 2, fine_y)[target]
    reaction_grid = reaction_sum.reshape(2, layer_count, inner_x, inner_y)
    coarse_accel = bond + reaction_grid
    coarse_velocity = coarse_vel + 0.5 * STEP * (coarse_acc + coarse_accel)
    fine_accel = chain_force(fine_new) + coupling
    fine_velocity = fine_vel + 0.5 * STEP * (fine_acc + fine_accel)
    return (coarse_accel, coarse_velocity, fine_accel, fine_velocity)


def solution(mesh):
    in_specs = (
        P(None, "slab", "patch", None),
        P(None, "slab", "patch", None),
        P(None, "slab", "patch", None),
        P("slab", "patch", None),
        P("slab", "patch", None),
        P(("patch", "slab"), None, None),
        P(("patch", "slab"), None, None),
        P(("patch", "slab"), None, None),
        P(("patch", "slab"), None),
        P(("patch", "slab")),
    )
    out_specs = (
        P(None, "slab", "patch", None),
        P(None, "slab", "patch", None),
        P(("patch", "slab"), None, None),
        P(("patch", "slab"), None, None),
    )
    return jax.shard_map(body, mesh=mesh, in_specs=in_specs, out_specs=out_specs, check_vma=False)
```

profile of v0, /device:TPU:1, one launch (start us, length us, event | category | flops | bytes accessed | tf_op | source)
XLA Modules:
  0.0 204.0 jit_solution(4966109457403561750)
XLA Ops:
  0.6 0.7 fusion.27
  1.5 0.8 select_reduce_fusion
  2.3 0.7 fusion.689
  3.0 1.0 scatter_custom_fusion
  4.0 0.8 all_to_all.12
  4.8 20.4 %all-to-all-start = ((s32[128,1,2]{2,1,0:T(1,128)}), s32[128,1,2]{2,1,0:T(1,128)S(1)}, u32[]{:S(2)}, u32[]{:S(2)}) async-start(s32[128,1,2]{2,1,0:T(1,128)} %bitcast.361), calls=%async_computation | async-start | bytes 131072 | tf_op jit(solution)/shard_map/all_to_all | solution.py:171
  25.2 0.8 convert_bitcast_fusion
  26.0 0.9 multiply_add_fusion.3
  26.9 3.5 %collective-permute-start = (f32[4,2,6,128]{3,2,1,0:T(8,128)S(1)}, f32[4,2,6,128]{3,2,1,0:T(8,128)S(1)}, u32[]{:S(2)}, u32[]{:S(2)}) collective-permute-start(f32[4,2,6,128]{3,2,1,0:T(8,128)S(1)} %get-tuple-element.135), channel_id=1, source_target_pairs={{0,4},{4,8},{8,12},{12,16},{16,20},{20,24},{24,28},{28,32},{32,36}... | collective-permute-start | bytes 73736 | tf_op jit(solution)/shard_map/ppermute | solution.py:17
  30.5 1.9 collective-permute-start.1
  32.4 0.6 fusion.4
  33.0 3.8 %collective-permute-start.2 = (f32[3,1,32,128]{3,2,1,0:T(8,128)}, f32[3,1,32,128]{3,2,1,0:T(8,128)}, u32[]{:S(2)}, u32[]{:S(2)}) collective-permute-start(f32[3,1,32,128]{3,2,1,0:T(8,128)} %get-tuple-element.137), channel_id=1, source_target_pairs={{0,1},{1,2},{2,3},{4,5},{5,6},{6,7},{8,9},{9,10},{10,11},{12,13},{... | collective-permute-start | bytes 147464 | tf_op jit(solution)/shard_map/ppermute | solution.py:17
  36.8 1.3 collective-permute-start.3
  38.1 1.3 multiply_add_fusion.1
  39.4 0.9 slice_subtract_fusion
  41.0 1.0 broadcast_in_dim.68
  42.0 9.5 %scatter_fusion = f32[256,2,256]{2,1,0:T(2,128)} fusion(f32[256,2,256]{2,1,0:T(2,128)} %broadcast_in_dim.68, s32[96]{0:T(128)S(1)} %fusion.689, f32[96,2,256]{2,1,0:T(2,128)S(1)} %multiply_add_fusion.1), kind=kCustom, calls=%fused_computation.3 | custom fusion | bytes 590208 | tf_op jit(solution)/shard_map/scatter | solution.py:162
  51.5 17.8 %all-to-all-start.1 = ((f32[128,2,2,256]{3,2,1,0:T(2,128)}), f32[128,2,2,256]{3,2,1,0:T(2,128)S(1)}, u32[]{:S(2)}, u32[]{:S(2)}) async-start(f32[128,2,2,256]{3,2,1,0:T(2,128)} %bitcast.367), calls=%async_computation.1 | async-start | bytes 1048576 | tf_op jit(solution)/shard_map/all_to_all | solution.py:164
  69.8 0.8 reduce.5
  70.8 1.0 gather_fusion
  73.7 15.5 %copy.34 = f32[256,2,128,2]{3,2,1,0:T(8,128)} copy(f32[256,2,128,2]{2,1,0,3:T(2,128)S(1)} %pad_maximum_fusion) | data formatting | bytes 1048576 | tf_op jit(solution)/shard_map/stack | solution.py:100
  89.3 0.7 ge.1087
  90.0 0.7 copy.33
  90.8 1.2 copy.30
  91.9 25.2 %reshape.1156 = f32[128,2,2,256]{3,2,1,0:T(2,128)} reshape(f32[256,2,128,2]{3,2,1,0:T(8,128)} %copy.34) | data formatting | bytes 1048576 | tf_op jit(solution)/shard_map/reshape | solution.py:101
  117.3 0.6 fusion.8
  118.0 0.6 fusion.28
  118.6 0.7 fusion.10
  119.3 0.7 fusion.29
  120.7 0.6 fusion.6
  122.0 0.7 fusion.5
  122.8 0.7 broadcast_compare_fusion.2
  123.5 0.7 fusion.31
  124.8 0.8 pad_maximum_fusion.2
  125.7 1.5 fusion.99
  127.2 2.2 %subtract_select_fusion = f32[128,2,2,256]{3,2,1,0:T(2,128)} fusion(f32[128,2,2,256]{3,2,1,0:T(2,128)} %reshape.1156, f32[128,2,2,256]{3,2,1,0:T(2,128)S(1)} %all-to-all-done.1, pred[128,2]{1,0:T(8,128)(4,1)} %copy.33), kind=kLoop, calls=%fused_computation.8 | loop fusion | flops 262144 | bytes 1573120 | tf_op jit(solution)/shard_map/jit(_where)/select_n | solution.py:180
  129.4 16.7 %all-to-all-start.2 = ((f32[128,2,2,256]{3,2,1,0:T(2,128)}), f32[128,2,2,256]{3,2,1,0:T(2,128)}, u32[]{:S(2)}, u32[]{:S(2)}) async-start(f32[128,2,2,256]{3,2,1,0:T(2,128)} %subtract_select_fusion), calls=%async_computation.2 | async-start | bytes 1048576 | tf_op jit(solution)/shard_map/all_to_all | solution.py:183
  146.0 0.8 multiply_divide_fusion
  146.8 0.7 compare_convert_fusion
  147.5 15.3 %fusion.79 = (f32[1,2,32,128]{3,2,1,0:T(8,128)}, f32[2,32,128]{2,1,0:T(8,128)S(1)}, f32[2,32,128]{2,1,0:T(8,128)S(1)}, f32[2,32,128]{2,1,0:T(8,128)S(1)}, f32[2,...) fusion(f32[3,1,32,128]{3,2,1,0:T(8,128)} %collective-permute-do, ...), kind=kLoop, calls=%fused_computation.149 | loop fusion | flops 14737408 | bytes 15224448 | tf_op jit(solution)/shard_map/stack | solution.py:147
  162.9 1.4 fusion.71
  164.3 1.8 fusion
  166.1 11.1 %slice.3611 = f32[256,2,128]{2,1,0:T(2,128)S(1)} slice(f32[256,2,256]{2,1,0:T(2,128)S(1)} %fusion), slice={[0:256:1], [0:2:1], [1:256:2]} | slice | bytes 524288 | tf_op jit(solution)/shard_map/slice | solution.py:106
  177.2 11.1 %slice.3610 = f32[256,2,128]{2,1,0:T(2,128)S(1)} slice(f32[256,2,256]{2,1,0:T(2,128)S(1)} %fusion), slice={[0:256:1], [0:2:1], [0:256:2]} | slice | bytes 524288 | tf_op jit(solution)/shard_map/slice | solution.py:105
  189.3 8.9 %scatter_fusion.1 = f32[2,64,128]{2,0,1:T(2,128)S(1)} fusion(f32[2,64,128]{2,0,1:T(2,128)S(1)} %broadcast_in_dim.65, s32[256]{0:T(256)} %bitcast.1893, f32[256,2,128]{2,1,0:T(2,128)S(1)} %add_negate_fusion), kind=kCustom, calls=%fused_computation.4 | custom fusion | flops 65536 | bytes 787456 | tf_op jit(solution)/shard_map/scatter-add | solution.py:182
  198.2 1.5 multiply_add_fusion.2
  199.7 2.0 gather_fusion.1
  201.7 2.3 %multiply_add_fusion = (f32[96,2,256]{2,1,0:T(2,128)}, f32[96,2,256]{2,1,0:T(2,128)}) fusion(f32[96,2,256]{2,1,0:T(2,128)} %param.16, f32[96,2,256]{2,1,0:T(2,128)} %param.17, f32[96,2,256]{2,1,0:T(2,128)S(1)} %gather_fusion.1, f32[96,2,255]{2,1,0:T(2,128)} %slice_subtract_fusion), kind=kLoop, calls=%fused_computation.15 | loop fusion | flops 245760 | bytes 1178880 | tf_op jit(solution)/shard_map/add | solution.py:195
  (62 shorter events, 6.5 us)
Async XLA Ops:
  4.8 46.7 %all-to-all-start = ((s32[128,1,2]{2,1,0:T(1,128)}), s32[128,1,2]{2,1,0:T(1,128)S(1)}, u32[]{:S(2)}, u32[]{:S(2)}) async-start(s32[128,1,2]{2,1,0:T(1,128)} %bitcast.361), calls=%async_computation | async-start | bytes 131072 | tf_op jit(solution)/shard_map/all_to_all | solution.py:171
  26.9 90.2 %collective-permute-start = (f32[4,2,6,128]{3,2,1,0:T(8,128)S(1)}, f32[4,2,6,128]{3,2,1,0:T(8,128)S(1)}, u32[]{:S(2)}, u32[]{:S(2)}) collective-permute-start(f32[4,2,6,128]{3,2,1,0:T(8,128)S(1)} %get-tuple-element.135), channel_id=1, source_target_pairs={{0,4},{4,8},{8,12},{12,16},{16,20},{20,24},{24,28},{28,32},{32,36}... | collective-permute-start | bytes 73736 | tf_op jit(solution)/shard_map/ppermute | solution.py:17
  30.5 86.7 %collective-permute-start.1 = (f32[4,2,6,128]{3,2,1,0:T(8,128)S(1)}, f32[4,2,6,128]{3,2,1,0:T(8,128)S(1)}, u32[]{:S(2)}, u32[]{:S(2)}) collective-permute-start(f32[4,2,6,128]{3,2,1,0:T(8,128)S(1)} %get-tuple-element.136), channel_id=1, source_target_pairs={{4,0},{8,4},{12,8},{16,12},{20,16},{24,20},{28,24},{32,28},{36,32}... | collective-permute-start | bytes 73736 | tf_op jit(solution)/shard_map/ppermute | solution.py:20
  33.0 113.0 %collective-permute-start.2 = (f32[3,1,32,128]{3,2,1,0:T(8,128)}, f32[3,1,32,128]{3,2,1,0:T(8,128)}, u32[]{:S(2)}, u32[]{:S(2)}) collective-permute-start(f32[3,1,32,128]{3,2,1,0:T(8,128)} %get-tuple-element.137), channel_id=1, source_target_pairs={{0,1},{1,2},{2,3},{4,5},{5,6},{6,7},{8,9},{9,10},{10,11},{12,13},{... | collective-permute-start | bytes 147464 | tf_op jit(solution)/shard_map/ppermute | solution.py:17
  36.8 109.2 %collective-permute-start.3 = (f32[3,1,32,128]{3,2,1,0:T(8,128)}, f32[3,1,32,128]{3,2,1,0:T(8,128)}, u32[]{:S(2)}, u32[]{:S(2)}) collective-permute-start(f32[3,1,32,128]{3,2,1,0:T(8,128)} %get-tuple-element.138), channel_id=1, source_target_pairs={{1,0},{2,1},{3,2},{5,4},{6,5},{7,6},{9,8},{10,9},{11,10},{13,12},{... | collective-permute-start | bytes 147464 | tf_op jit(solution)/shard_map/ppermute | solution.py:20
  51.5 75.7 %all-to-all-start.1 = ((f32[128,2,2,256]{3,2,1,0:T(2,128)}), f32[128,2,2,256]{3,2,1,0:T(2,128)S(1)}, u32[]{:S(2)}, u32[]{:S(2)}) async-start(f32[128,2,2,256]{3,2,1,0:T(2,128)} %bitcast.367), calls=%async_computation.1 | async-start | bytes 1048576 | tf_op jit(solution)/shard_map/all_to_all | solution.py:164
  70.8 1.7 copy-start.5
  117.2 4.4 %copy-start.3 = (f32[4,2,6,128]{3,2,1,0:T(8,128)}, f32[4,2,6,128]{3,2,1,0:T(8,128)S(1)}, u32[]{:S(2)}) copy-start(f32[4,2,6,128]{3,2,1,0:T(8,128)S(1)} %collective-permute-done) | copy-start | bytes 73732
  117.2 4.4 %copy-start.4 = (f32[4,2,6,128]{3,2,1,0:T(8,128)}, f32[4,2,6,128]{3,2,1,0:T(8,128)S(1)}, u32[]{:S(2)}) copy-start(f32[4,2,6,128]{3,2,1,0:T(8,128)S(1)} %collective-permute-done.1) | copy-start | bytes 73732
  121.9 3.8 %copy-start = (f32[4,2,44,124]{3,2,1,0:T(8,128)}, f32[4,2,44,124]{3,2,1,0:T(8,128)S(1)}, u32[]{:S(2)}) copy-start(f32[4,2,44,124]{3,2,1,0:T(8,128)S(1)} %get-tuple-element.124) | copy-start | bytes 523780
  122.0 3.6 %copy-start.1 = (f32[4,2,44,126]{3,2,1,0:T(8,128)}, f32[4,2,44,126]{3,2,1,0:T(8,128)S(1)}, u32[]{:S(2)}) copy-start(f32[4,2,44,126]{3,2,1,0:T(8,128)S(1)} %get-tuple-element.127) | copy-start | bytes 532228
  124.6 1.1 copy-start.2
  129.4 70.4 %all-to-all-start.2 = ((f32[128,2,2,256]{3,2,1,0:T(2,128)}), f32[128,2,2,256]{3,2,1,0:T(2,128)}, u32[]{:S(2)}, u32[]{:S(2)}) async-start(f32[128,2,2,256]{3,2,1,0:T(2,128)} %subtract_select_fusion), calls=%async_computation.2 | async-start | bytes 1048576 | tf_op jit(solution)/shard_map/all_to_all | solution.py:183
where the time goes:
time: 207 us; the launch traced here: 204 us
  local copies, waits for them, and re-layouts  85 us (41%)
  starting transfers between devices  65.4 us (32%)
  other arithmetic  52.5 us (25%)
    reshape x2, local copies, waits for them, and re-layouts, refine_row(): return joined.reshape(coarse_rows.shape[:-1] + (2 * coarse_rows.shape[-1],))  26.4 us
    all_to_all x1, starting transfers between devices, body(): lax.all_to_all(send_anchor.reshape(patches, capacity), 'patch', split_axi...  20.4 us
    all_to_all x1, starting transfers between devices, body(): lax.all_to_all(send_disp.reshape(patches, capacity, 2, fine_y), 'patch',...  17.8 us
    another operation x2, other arithmetic, body(): bond = jnp.stack([force_x + layer_x, force_y + layer_y])  16.7 us
    all_to_all x1, starting transfers between devices, body(): lax.all_to_all(answer.reshape(patches, capacity, 2, fine_y), 'patch', spl...  16.7 us
    another operation x2, local copies, waits for them, and re-layouts, refine_row(): joined = jnp.stack([coarse_rows, middle], axis=-1)  15.9 us
    slice x1, local copies, waits for them, and re-layouts, restrict_row(): even_part = values[..., 0::2]  11.1 us
    slice x1, local copies, waits for them, and re-layouts, restrict_row(): odd_part = values[..., 1::2]  11.1 us
  transfers between devices with their start and end apart: 7, of which 0 were waited for; matrix products, arithmetic and copies ran while one was open for 63% of the time, Pallas kernels for 0%

commit v1 on v0

v1 whole, which is shorter than its diff:
```python
import jax
import jax.numpy as jnp
from jax import lax
from jax.experimental import pallas as pl
from jax.experimental.pallas import tpu as pltpu
from jax.sharding import PartitionSpec as P

RADIUS = 6
STEP = 0.5
F32 = jnp.float32
BF16 = jnp.bfloat16
I32 = jnp.int32


def iota(shape, dim):
    return lax.broadcasted_iota(I32, shape, dim)


def place(patch, patches):
    if patches != 128:
        return patch
    return patch ^ 80


def split3(x):
    high = x.astype(BF16)
    rest = x - high.astype(F32)
    mid = rest.astype(BF16)
    low = (rest - mid.astype(F32)).astype(BF16)
    return (high, mid, low)


def dot(a, b):
    return jnp.dot(a, b, preferred_element_type=F32)


def dot_ta(a, b):
    return lax.dot_general(a, b, (((0,), (0,)), ((), ())), preferred_element_type=F32)


def refine_weights(cell, point, cells):
    half = point >> 1
    same = (cell == half).astype(F32)
    after = (cell == jnp.minimum(half + 1, cells - 1)).astype(F32)
    return jnp.where((point & 1) == 0, same, 0.5 * (same + after)).astype(BF16)


def fine_plane(refs, half, comp, blocks):
    rows = pl.ds(half * 2 + comp, blocks, stride=4)
    disp, vel, acc = [ref[rows, :] for ref in refs]
    return disp + STEP * vel + (0.5 * STEP * STEP) * acc, vel, acc


def rank_row(owner_col, owner_row, blocks):
    earlier = iota((blocks, blocks), 0) < iota((blocks, blocks), 1)
    return jnp.sum(((owner_col == owner_row) & earlier).astype(I32), axis=0, keepdims=True)


def rank_col(owner_col, owner_row, blocks):
    earlier = iota((blocks, blocks), 1) < iota((blocks, blocks), 0)
    return jnp.sum(((owner_col == owner_row) & earlier).astype(I32), axis=1, keepdims=True)


def to_col(row, blocks):
    same = iota((blocks, blocks), 0) == iota((blocks, blocks), 1)
    return jnp.sum(jnp.where(same, row, 0), axis=1, keepdims=True)


def slot_choice(owner, blocks, patches):
    owner_row = place(owner[...], patches)
    owner_col = to_col(owner_row, blocks)
    rank = rank_row(owner_col, owner_row, blocks)
    slot = iota((2 * patches, blocks), 0)
    return (owner_row == slot % patches) & (rank == slot // patches)


def load_all(pairs, sems):
    copies = [
        pltpu.make_async_copy(source, target, sems.at[n]) for n, (source, target) in enumerate(pairs)
    ]
    for copy in copies:
        copy.start()
    return copies


def pack_kernel(
    blocks, patches, cells, owner_in, anchor_in, fd_in, fv_in, fa_in, send,
    owner, anchor, fd, fv, fa, sems,
):
    copies = load_all(
        ((owner_in, owner), (anchor_in, anchor), (fd_in, fd), (fv_in, fv), (fa_in, fa)), sems
    )
    points = 2 * cells
    weights = refine_weights(iota((points, cells), 1), iota((points, cells), 0), cells)
    for copy in copies[:2]:
        copy.wait()
    chosen = slot_choice(owner, blocks, patches)
    named = jnp.sum(jnp.where(chosen, anchor[...] + 1, 0), axis=1, keepdims=True).astype(F32)
    lane = iota((patches, 128), 1)
    send[pl.ds(NAMES, patches, stride=OUT_ROWS), :] = jnp.where(
        lane == 0, named[:patches], jnp.where(lane == 1, named[patches:], 0.0)
    )
    onehot = chosen.astype(F32).astype(BF16)
    for copy in copies[2:]:
        copy.wait()
    planes = []
    for comp in range(2):
        parts = [fine_plane((fd, fv, fa), half, comp, blocks)[0] for half in range(2)]
        planes.append(jnp.concatenate(parts, axis=1))
    fine_new = jnp.concatenate(planes, axis=0)
    restricted = sum(dot(part, weights) for part in split3(fine_new))
    by_block = jnp.concatenate([restricted[:blocks], restricted[blocks:]], axis=1)
    put_slots(send, OUT_ROWS, sum(dot(onehot, part) for part in split3(by_block)), patches, cells)


OUT_ROWS = 5
NAMES = 4
BACK_ROWS = 4


def put_slots(ref, stride, value, patches, cells):
    for k in range(2):
        for comp in range(2):
            ref[pl.ds(k * 2 + comp, patches, stride=stride), :] = value[
                k * patches : (k + 1) * patches, comp * cells : (comp + 1) * cells
            ]


def get_slots(ref, stride, patches):
    slots = []
    for k in range(2):
        rows = [pl.ds(k * 2 + comp, patches, stride=stride) for comp in range(2)]
        slots.append(jnp.concatenate([ref[at, :] for at in rows], axis=1))
    return jnp.concatenate(slots, axis=0)


def slot_rows(got, patches, rows):
    names = got[pl.ds(NAMES, patches, stride=OUT_ROWS), :]
    row = (iota((patches, rows), 1) + 1).astype(F32)
    parts = [(names[:, k : k + 1] == row).astype(F32).astype(BF16) for k in range(2)]
    return jnp.concatenate(parts, axis=0)


def rows_kernel(patches, cells, rows, got, new, send):
    onehot = slot_rows(got, patches, rows)
    grid = jnp.concatenate([new[:rows, :], new[rows:, :]], axis=1)
    put_slots(send, BACK_ROWS, sum(dot(onehot, part) for part in split3(grid)), patches, cells)


def coarse_kernel(patches, cells, rows, got, coarse, bond, vel, acc, accel_out, velocity_out):
    onehot = slot_rows(got, patches, rows)
    summed = sum(dot_ta(onehot, part) for part in split3(get_slots(got, OUT_ROWS, patches)))
    count = dot_ta(onehot, jnp.ones((2 * patches, cells), BF16))
    lane = iota((rows, cells), 1)
    for comp in range(2):
        own = slice(comp * rows, (comp + 1) * rows)
        row = coarse[own, :]
        after = jnp.where(lane == cells - 1, row, pltpu.roll(row, cells - 1, 1))
        odd = 0.5 * (row + after)
        before = jnp.where(lane == 0, 0.0, pltpu.roll(odd, 1, 1))
        ending = jnp.where(lane == cells - 1, odd, 0.0)
        folded = row + 0.5 * odd + 0.5 * (before + ending)
        reaction = summed[:, comp * cells : (comp + 1) * cells] - count * folded
        accel = bond[own, :] + reaction
        accel_out[own, :] = accel
        velocity_out[own, :] = vel[own, :] + 0.5 * STEP * (acc[own, :] + accel)


def fine_own_kernel(blocks, patches, fd, fv, fa, owner, accel_base, velocity_base, fine_onehot):
    owner_row = place(owner[...], patches)
    owner_col = to_col(owner_row, blocks)
    rank = rank_col(owner_col, owner_row, blocks)
    slot = iota((blocks, 2 * patches), 1)
    chosen = (owner_col == slot % patches) & (rank == slot // patches)
    fine_onehot[...] = chosen.astype(F32).astype(BF16)
    lane = iota((blocks, 128), 1)
    for comp in range(2):
        (x0, v0, a0), (x1, v1, a1) = [
            fine_plane((fd, fv, fa), half, comp, blocks) for half in range(2)
        ]
        up0, up1 = pltpu.roll(x0, 127, 1), pltpu.roll(x1, 127, 1)
        down0, down1 = pltpu.roll(x0, 1, 1), pltpu.roll(x1, 1, 1)
        next0, next1 = jnp.where(lane == 127, up1, up0), jnp.where(lane == 127, x1, up1)
        prev0, prev1 = jnp.where(lane == 0, x0, down0), jnp.where(lane == 0, down0, down1)
        for half, x, v, a, after, before in (
            (0, x0, v0, a0, next0, prev0),
            (1, x1, v1, a1, next1, prev1),
        ):
            at = pl.ds(half * 2 + comp, blocks, stride=4)
            base = (after - x) - (x - before) - x
            accel_base[at, :] = base
            velocity_base[at, :] = v + 0.5 * STEP * (a + base)


def finish_kernel(
    blocks, patches, cells, got, accel_base, velocity_base, fine_onehot, accel_out, velocity_out
):
    onehot = fine_onehot[...]
    points = 2 * cells
    weights = refine_weights(iota((cells, points), 0), iota((cells, points), 1), cells)
    refined = jnp.zeros((2 * blocks, points), F32)
    for part in split3(get_slots(got, BACK_ROWS, patches)):
        taken = dot(onehot, part).astype(BF16)
        taken = jnp.concatenate([taken[:, :cells], taken[:, cells:]], axis=0)
        refined = refined + dot(taken, weights)
    for comp in range(2):
        for half in range(2):
            at = pl.ds(half * 2 + comp, blocks, stride=4)
            added = refined[comp * blocks : (comp + 1) * blocks, half * 128 : (half + 1) * 128]
            accel_out[at, :] = accel_base[at, :] + added
            velocity_out[at, :] = velocity_base[at, :] + 0.5 * STEP * added


def prepare_kernel(inner_x, disp, vel, acc, horizon, crack, new, low, high, below, above):
    rows = 2 * inner_x
    value = disp[...] + STEP * vel[...] + (0.5 * STEP * STEP) * acc[...]
    new[...] = value
    fields = (value[:rows], value[rows:], horizon[...].astype(F32), crack[...].astype(F32))
    for f, field in enumerate(fields):
        for layer in range(2):
            at = (f * 2 + layer) * RADIUS
            begin, end = layer * inner_x, (layer + 1) * inner_x
            low[at : at + RADIUS, :] = field[end - RADIUS : end]
            high[at : at + RADIUS, :] = field[begin : begin + RADIUS]
        if f < 3:
            below[f * inner_x : (f + 1) * inner_x, :] = field[inner_x:]
            above[f * inner_x : (f + 1) * inner_x, :] = field[:inner_x]


def bond_offsets(radius):
    listing = {}
    for along_y in range(-radius, radius + 1):
        for along_x in range(-radius, radius + 1):
            square = along_x * along_x + along_y * along_y
            if 0 < square <= radius * radius:
                level = 2
                while level * level < square:
                    level += 1
                listing.setdefault(along_y, []).append((along_x, square, level))
    return listing


def micro_of(horizon):
    present = horizon > 0.0
    guard = jnp.where(present, horizon, 1.0)
    return jnp.where(present, 2.0 / (guard * guard), 0.0)


FIELDS = 8
LEVELS = (2, 3, 4, 5, 6)


def bond_kernel(inner_x, new, horizon, crack, low, high, below, above, out, wide, moved, there):
    rows = 2 * inner_x
    cells = 128
    extent = inner_x + 2 * RADIUS
    for layer in range(2):
        begin = layer * inner_x
        for f in range(4):
            at = (f * 2 + layer) * RADIUS
            wide[f, layer, 0:RADIUS, :] = low[at : at + RADIUS, :]
            wide[f, layer, RADIUS + inner_x : extent, :] = high[at : at + RADIUS, :]
        middle = slice(RADIUS, RADIUS + inner_x)
        wide[0, layer, middle, :] = new[begin : begin + inner_x, :]
        wide[1, layer, middle, :] = new[rows + begin : rows + begin + inner_x, :]
        wide[2, layer, middle, :] = horizon[begin : begin + inner_x, :].astype(F32)
        wide[3, layer, middle, :] = crack[begin : begin + inner_x, :].astype(F32)
    for r in range(8 + 2 * RADIUS):
        fields = [
            jnp.concatenate(
                [wide[f, layer, pl.ds(r, 4, stride=8), :] for layer in range(2)], axis=0
            )
            for f in range(4)
        ]
        reach = fields[2]
        micro = micro_of(reach)
        there[r] = (reach > 0.0).astype(F32)
        moved[RADIUS, 0, r] = fields[0]
        moved[RADIUS, 1, r] = fields[1]
        moved[RADIUS, 2, r] = fields[3]
        for n, level in enumerate(LEVELS):
            moved[RADIUS, 3 + n, r] = jnp.where(reach >= float(level), micro, 0.0)

    def shift_row(r, carry):
        for f in range(FIELDS):
            field = moved[RADIUS, f, r]
            for along_y in range(-RADIUS, RADIUS + 1):
                if along_y != 0:
                    moved[RADIUS + along_y, f, r] = pltpu.roll(field, (-along_y) % cells, 1)
        return carry

    lax.fori_loop(0, 8 + 2 * RADIUS, shift_row, 0)
    lane = iota((8, cells), 1)
    offsets = bond_offsets(RADIUS)

    def force_row(i, carry):
        own = [moved[RADIUS, f, i + RADIUS] for f in range(FIELDS)]
        force_x = jnp.zeros((8, cells), F32)
        force_y = jnp.zeros((8, cells), F32)
        for along_y in range(-RADIUS, RADIUS + 1):
            sum_x = jnp.zeros((8, cells), F32)
            sum_y = jnp.zeros((8, cells), F32)
            for along_x, square, level in offsets[along_y]:
                r = i + (RADIUS + along_x)
                at = RADIUS + along_y
                scale = 1.0 / float(square) ** 1.5
                weight = (own[1 + level] + moved[at, 1 + level, r]) * (
                    there[r] - own[2] * moved[at, 2, r]
                )
                stretch = 0.0
                if along_x:
                    stretch = (scale * along_x) * (moved[at, 0, r] - own[0])
                if along_y:
                    stretch = stretch + (scale * along_y) * (moved[at, 1, r] - own[1])
                term = weight * stretch
                if along_x:
                    sum_x = sum_x + float(along_x) * term
                sum_y = sum_y + term
            if along_y:
                inside = (lane + along_y >= 0) & (lane + along_y < cells)
                sum_x = jnp.where(inside, sum_x, 0.0)
                sum_y = jnp.where(inside, sum_y, 0.0)
                force_y = force_y + float(along_y) * sum_y
            force_x = force_x + sum_x
        wide[0, 0, pl.ds(8 * i, 8), :] = force_x
        wide[1, 0, pl.ds(8 * i, 8), :] = force_y
        return carry

    lax.fori_loop(0, 8, force_row, 0)
    reach = horizon[...].astype(F32)
    micro = micro_of(reach)
    for comp in range(2):
        own = new[comp * rows : (comp + 1) * rows, :]
        force = jnp.zeros((rows, cells), F32)
        for side in range(2):
            far = (below, above)[side]

            def beside(mine, f):
                outer = far[f * inner_x : (f + 1) * inner_x, :]
                if side == 0:
                    return jnp.concatenate([outer, mine[:inner_x]], axis=0)
                return jnp.concatenate([mine[inner_x:], outer], axis=0)

            reach_j = beside(reach, 2)
            factor = jnp.where(reach_j > 0.0, micro + micro_of(reach_j), 0.0)
            force = force + factor * (beside(own, comp) - own)
        out[comp * rows : (comp + 1) * rows, :] = force
    for comp in range(2):
        for i in range(8):
            at = pl.ds(comp * rows + i, 8, stride=8)
            out[at, :] = out[at, :] + wide[comp, 0, 8 * i : 8 * i + 8, :]


def shape(*dims, dtype=F32):
    return jax.ShapeDtypeStruct(dims, dtype)


def call(kernel, out_shape, name, flops, traffic, scratch=(), vmem=None, in_specs=None):
    extra = {} if in_specs is None else {"in_specs": in_specs}
    return pl.pallas_call(
        kernel,
        out_shape=out_shape,
        name=name,
        scratch_shapes=list(scratch),
        compiler_params=pltpu.CompilerParams(vmem_limit_bytes=vmem or 16 * 2**20),
        cost_estimate=pl.CostEstimate(flops=flops, bytes_accessed=traffic, transcendentals=0),
        **extra,
    )


def fine_view(x):
    blocks = x.shape[0]
    return x.reshape(blocks, 2, 2, 128).transpose(0, 2, 1, 3).reshape(blocks * 4, 128)


def fine_unview(x):
    blocks = x.shape[0] // 4
    return x.reshape(blocks, 2, 2, 128).transpose(0, 2, 1, 3).reshape(blocks, 2, 256)


def exchange(x, patches):
    order = sorted(range(patches), key=lambda patch: place(patch, patches))
    return lax.all_to_all(
        x, "patch", split_axis=0, concat_axis=0, tiled=True, axis_index_groups=[order]
    )


def body(
    coarse_disp,
    coarse_vel,
    coarse_acc,
    horizon,
    crack_flag,
    fine_disp,
    fine_vel,
    fine_acc,
    fine_owner,
    fine_anchor,
):
    _, layers, inner_x, cells = coarse_disp.shape
    rows = layers * inner_x
    blocks = fine_disp.shape[0]
    patches = lax.axis_size("patch")
    slabs = lax.axis_size("slab")
    fine = [fine_view(x) for x in (fine_disp, fine_vel, fine_acc)]
    owner = fine_owner.reshape(1, blocks)
    anchor = fine_anchor.reshape(1, blocks)
    grid = [x.reshape(2 * rows, cells) for x in (coarse_disp, coarse_vel, coarse_acc)]
    reach = horizon.reshape(rows, cells)
    crack = crack_flag.reshape(rows, cells)

    send = call(
        lambda *refs: pack_kernel(blocks, patches, cells, *refs),
        shape(OUT_ROWS * patches, cells),
        "pack_fine",
        2 * 10**6,
        10**6,
        scratch=(
            pltpu.VMEM(owner.shape, I32),
            pltpu.VMEM(anchor.shape, I32),
            *[pltpu.VMEM(x.shape, F32) for x in fine],
            pltpu.SemaphoreType.DMA((5,)),
        ),
        in_specs=[pl.BlockSpec(memory_space=pltpu.HBM)] * 5,
        vmem=60 * 2**20,
    )(owner, anchor, *fine)
    send, grid, reach, crack = lax.optimization_barrier((send, grid, reach, crack))
    got = exchange(send.reshape(patches, 1, OUT_ROWS * cells), patches)
    got = got.reshape(OUT_ROWS * patches, cells)

    new, low, high, below, above = call(
        lambda *refs: prepare_kernel(inner_x, *refs),
        (
            shape(2 * rows, cells),
            shape(8 * RADIUS, cells),
            shape(8 * RADIUS, cells),
            shape(3 * inner_x, cells),
            shape(3 * inner_x, cells),
        ),
        "prepare_coarse",
        10**6,
        10**6,
    )(*grid, reach, crack)
    up = [(i, i + 1) for i in range(patches - 1)]
    down = [(i + 1, i) for i in range(patches - 1)]
    low, high = lax.ppermute(low, "patch", up), lax.ppermute(high, "patch", down)
    up = [(i, i + 1) for i in range(slabs - 1)]
    down = [(i + 1, i) for i in range(slabs - 1)]
    below, above = lax.ppermute(below, "slab", up), lax.ppermute(above, "slab", down)

    got, low, high, below, above = lax.optimization_barrier((got, low, high, below, above))
    send = call(
        lambda *refs: rows_kernel(patches, cells, rows, *refs),
        shape(BACK_ROWS * patches, cells),
        "take_rows",
        2 * 10**6,
        10**6,
    )(got, new)
    send, new, reach, crack, fine, owner = lax.optimization_barrier(
        (send, new, reach, crack, fine, owner)
    )
    returned = exchange(send.reshape(patches, BACK_ROWS, cells), patches)
    returned = returned.reshape(BACK_ROWS * patches, cells)

    span = 8 + 2 * RADIUS
    bond = call(
        lambda *refs: bond_kernel(inner_x, *refs),
        shape(2 * rows, cells),
        "bond_force",
        10**9,
        10**7,
        scratch=(
            pltpu.VMEM((4, 2, 64, cells), F32),
            pltpu.VMEM((2 * RADIUS + 1, FIELDS, span, 8, cells), F32),
            pltpu.VMEM((span, 8, cells), F32),
        ),
        vmem=32 * 2**20,
    )(new, reach, crack, low, high, below, above)

    coarse_accel, coarse_velocity = call(
        lambda *refs: coarse_kernel(patches, cells, rows, *refs),
        (shape(2 * rows, cells), shape(2 * rows, cells)),
        "coarse_out",
        10**7,
        10**6,
    )(got, new, bond, grid[1], grid[2])
    fine_base = call(
        lambda *refs: fine_own_kernel(blocks, patches, *refs),
        (
            shape(4 * blocks, 128),
            shape(4 * blocks, 128),
            shape(blocks, 2 * patches, dtype=BF16),
        ),
        "fine_own",
        10**7,
        10**6,
    )(*fine, owner)
    fine_accel, fine_velocity = call(
        lambda *refs: finish_kernel(blocks, patches, cells, *refs),
        (shape(4 * blocks, 128), shape(4 * blocks, 128)),
        "finish",
        10**6,
        10**6,
    )(returned, *fine_base)
    return (
        coarse_accel.reshape(coarse_disp.shape),
        coarse_velocity.reshape(coarse_disp.shape),
        fine_unview(fine_accel),
        fine_unview(fine_velocity),
    )


def solution(mesh):
    in_specs = (
        P(None, "slab", "patch", None),
        P(None, "slab", "patch", None),
        P(None, "slab", "patch", None),
        P("slab", "patch", None),
        P("slab", "patch", None),
        P(("patch", "slab"), None, None),
        P(("patch", "slab"), None, None),
        P(("patch", "slab"), None, None),
        P(("patch", "slab"), None),
        P(("patch", "slab")),
    )
    out_specs = (
        P(None, "slab", "patch", None),
        P(None, "slab", "patch", None),
        P(("patch", "slab"), None, None),
        P(("patch", "slab"), None, None),
    )
    return jax.shard_map(body, mesh=mesh, in_specs=in_specs, out_specs=out_specs, check_vma=False)
```

time: 207 us -> 74.3 us (0.36); the launches traced: 204 us -> 73.9 us
  local copies, waits for them, and re-layouts: 85 us -> 0.14 us
  other arithmetic: 52.5 us -> 0 us
  starting transfers between devices: 65.4 us -> 50.8 us
  Pallas kernels: 0 us -> 11 us
  waiting for transfers between devices: 0.02 us -> 11 us
    reshape x3 -> x0, local copies, waits for them, and re-layouts: 26.5 us -> none  [the longest x2 26.4 us: refine_row(): return joined.reshape(coarse_rows.shape[:-1] + (2 * coarse_rows.shape[-1],))]
    slice x11 -> x0, local copies, waits for them, and re-layouts: 23.9 us -> none  [the longest x1 11.1 us: restrict_row(): even_part = values[..., 0::2]]
    another operation x7 -> x0, other arithmetic: 18.9 us -> none  [the longest x2 16.7 us: body(): bond = jnp.stack([force_x + layer_x, force_y + layer_y])]
    another operation x2 -> x0, local copies, waits for them, and re-layouts: 15.9 us -> none  [refine_row(): joined = jnp.stack([coarse_rows, middle], axis=-1)]
    all_to_all x3 -> x2, starting transfers between devices: 54.8 us -> 41.7 us  [exchange(): lax.all_to_all(x, 'patch', split_axis=0, concat_axis=0, tiled=True, axis_...]
    pallas_call x0 -> x7, Pallas kernels: none -> 11 us  [the longest x1 5.07 us: body(): call(lambda *refs: bond_kernel(inner_x, *refs), shape(2 * rows, cells), '...]
    scatter x2 -> x0, local copies, waits for them, and re-layouts: 10.5 us -> none  [the longest x1 9.52 us: body(): jnp.zeros((slot_count, 2, fine_y), jnp.float32).at[target].set(fine_new)]
    scatter-add x1 -> x0, other arithmetic: 8.9 us -> none  [body(): jnp.zeros_like(flat_grid).at[:, picked, :].add(reaction_slots)]
  transfers between devices with their start and end apart: 7 -> 6, of which waited for: 0 -> 3; matrix products, arithmetic and copies ran while one was open for 63% -> 0% of each run, Pallas kernels for 0% -> 9%
where the time goes in v1:
time: 74.3 us; the launch traced here: 73.9 us
  starting transfers between devices  50.8 us (68%)
  Pallas kernels  11 us (15%)
  waiting for transfers between devices  11 us (15%)
  between operations  0.83 us (1%)
    all_to_all x2, starting transfers between devices, exchange(): lax.all_to_all(x, 'patch', split_axis=0, concat_axis=0, tiled=True, axis_...  41.7 us
    all_to_all x2, waiting for transfers between devices, exchange(): lax.all_to_all(x, 'patch', split_axis=0, concat_axis=0, tiled=True, axis_...  5.28 us
    pallas_call x1, Pallas kernels, body(): call(lambda *refs: bond_kernel(inner_x, *refs), shape(2 * rows, cells), '...  5.07 us
    ppermute x1, waiting for transfers between devices, body(): lax.ppermute(low, 'patch', up)  4.86 us
    ppermute x1, starting transfers between devices, body(): lax.ppermute(below, 'slab', up)  3.2 us
    ppermute x1, starting transfers between devices, body(): lax.ppermute(low, 'patch', up)  2.73 us
    pallas_call x1, Pallas kernels, body(): call(lambda *refs: pack_kernel(blocks, patches, cells, *refs), shape(OUT_...  2.43 us
    ppermute x1, starting transfers between devices, body(): lax.ppermute(high, 'patch', down)  1.92 us
  transfers between devices with their start and end apart: 6, of which 3 were waited for; matrix products, arithmetic and copies ran while one was open for 0% of the time, Pallas kernels for 9%

profile of v1, /device:TPU:1, one launch (start us, length us, event | category | flops | bytes accessed | tf_op | source)
XLA Modules:
  0.0 73.9 jit_solution(1163007121688639506)
XLA Ops:
  0.6 2.4 %pack_fine.1 = f32[640,128]{1,0:T(8,128)} custom-call(s32[1,96]{1,0:T(1,128)} %bitcast.56, s32[1,96]{1,0:T(1,128)} %bitcast.59, f32[384,128]{1,0:T(8,128)} %bitcast.41, f32[384,128]{1,0:T(8,128)} %bitcast.43, f32[384,128]{1,0:T(8,128)} %bitcast.45), custom_call_target="tpu_custom_call" | custom-call | flops 2000000 | bytes 1000000 | tf_op jit(solution)/shard_map/pack_fine/pallas_call | solution.py:412
  3.1 0.0 copy-start.3
  3.1 0.0 copy-start.4
  3.1 0.0 copy-start.5
  3.1 0.0 copy-start.6
  3.1 0.0 copy-start.7
  3.1 25.0 %all-to-all-start = ((f32[128,1,640]{2,1,0:T(1,128)}), f32[128,1,640]{2,1,0:T(1,128)S(1)}, u32[]{:S(2)}, u32[]{:S(2)}) async-start(f32[128,1,640]{2,1,0:T(1,128)} %bitcast.58), calls=%async_computation | async-start | bytes 655360 | tf_op jit(solution)/shard_map/all_to_all | solution.py:383
  28.1 0.0 copy-done.3
  28.1 0.0 copy-done.4
  28.1 0.0 copy-done.5
  28.2 0.0 copy-done.6
  28.2 0.0 copy-done.7
  28.2 3.2 %collective-permute-start.2 = (f32[96,128]{1,0:T(8,128)S(1)}, f32[96,128]{1,0:T(8,128)S(1)}, u32[]{:S(2)}, u32[]{:S(2)}) collective-permute-start(f32[96,128]{1,0:T(8,128)S(1)} %get-tuple-element.43), channel_id=1, source_target_pairs={{0,1},{1,2},{2,3},{4,5},{5,6},{6,7},{8,9},{9,10},{10,11},{12,13},{... | collective-permute-start | bytes 147464 | tf_op jit(solution)/shard_map/ppermute | solution.py:449
  31.4 1.3 %collective-permute-start.3 = (f32[96,128]{1,0:T(8,128)S(1)}, f32[96,128]{1,0:T(8,128)S(1)}, u32[]{:S(2)}, u32[]{:S(2)}) collective-permute-start(f32[96,128]{1,0:T(8,128)S(1)} %get-tuple-element.44), channel_id=1, source_target_pairs={{1,0},{2,1},{3,2},{5,4},{6,5},{7,6},{9,8},{10,9},{11,10},{13,12},{... | collective-permute-start | bytes 147464 | tf_op jit(solution)/shard_map/ppermute | solution.py:449
  32.7 2.7 %collective-permute-start = (f32[48,128]{1,0:T(8,128)S(1)}, f32[48,128]{1,0:T(8,128)S(1)}, u32[]{:S(2)}, u32[]{:S(2)}) collective-permute-start(f32[48,128]{1,0:T(8,128)S(1)} %get-tuple-element.41), channel_id=1, source_target_pairs={{0,4},{4,8},{8,12},{12,16},{16,20},{20,24},{24,28},{28,32},{32,36}... | collective-permute-start | bytes 73736 | tf_op jit(solution)/shard_map/ppermute | solution.py:446
  35.5 1.9 %collective-permute-start.1 = (f32[48,128]{1,0:T(8,128)S(1)}, f32[48,128]{1,0:T(8,128)S(1)}, u32[]{:S(2)}, u32[]{:S(2)}) collective-permute-start(f32[48,128]{1,0:T(8,128)S(1)} %get-tuple-element.42), channel_id=1, source_target_pairs={{4,0},{8,4},{12,8},{16,12},{20,16},{24,20},{28,24},{32,28},{36,32}... | collective-permute-start | bytes 73736 | tf_op jit(solution)/shard_map/ppermute | solution.py:446
  37.4 4.9 %collective-permute-done.refs_3_ = f32[48,128]{1,0:T(8,128)S(1)} collective-permute-done((f32[48,128]{1,0:T(8,128)S(1)}, f32[48,128]{1,0:T(8,128)S(1)}, u32[]{:S(2)}, u32[]{:S(2)}) %collective-permute-start) | collective-permute-done | bytes 24608 | tf_op jit(solution)/shard_map/ppermute | solution.py:446
  42.2 0.9 %collective-permute-done.1.refs_4_ = f32[48,128]{1,0:T(8,128)S(1)} collective-permute-done((f32[48,128]{1,0:T(8,128)S(1)}, f32[48,128]{1,0:T(8,128)S(1)}, u32[]{:S(2)}, u32[]{:S(2)}) %collective-permute-start.1) | collective-permute-done | bytes 24608 | tf_op jit(solution)/shard_map/ppermute | solution.py:446
  43.1 0.0 collective-permute-done.2.refs_5_
  43.1 0.0 collective-permute-done.3.refs_6_
  43.1 0.0 all-to-all-done
  43.2 1.0 %take_rows.1 = f32[512,128]{1,0:T(8,128)} custom-call(f32[640,128]{1,0:T(8,128)S(1)} %bitcast.38, f32[128,128]{1,0:T(8,128)S(1)} %get-tuple-element.47.refs_1_.refs_0_), custom_call_target="tpu_custom_call" | custom-call | flops 2000000 | bytes 1000000 | tf_op jit(solution)/shard_map/take_rows/pallas_call | solution.py:452
  44.2 16.7 %all-to-all-start.1 = ((f32[128,4,128]{2,1,0:T(4,128)}), f32[128,4,128]{2,1,0:T(4,128)S(1)}, u32[]{:S(2)}, u32[]{:S(2)}) async-start(f32[128,4,128]{2,1,0:T(4,128)} %bitcast.26), calls=%async_computation.1 | async-start | bytes 524288 | tf_op jit(solution)/shard_map/all_to_all | solution.py:383
  60.9 0.0 copy-start.8
  60.9 5.1 %bond_force.1.refs_2_ = f32[128,128]{1,0:T(8,128)S(1)} custom-call(f32[128,128]{1,0:T(8,128)S(1)} %get-tuple-element.47.refs_1_.refs_0_, s32[64,128]{1,0:T(8,128)S(1)} %bitcast.53, s32[64,128]{1,0:T(8,128)S(1)} %bitcast.55, f32[48,128]{1,0:T(8,128)S(1)} %collective-permute-done.refs_3_, f32[48,128]{1,0:T(8,128)S(1)} %collective-permute-done.1.refs_4_, ...), custom_call_target="tpu_custom_call" | custom-call | flops 1000000000 | bytes 10000000 | tf_op jit(solution)/shard_map/bond_force/pallas_call | solution.py:466
  65.9 0.0 copy-start
  66.0 0.0 copy-start.1
  66.0 0.0 copy-start.2
  66.0 1.0 %coarse_out.1 = (f32[128,128]{1,0:T(8,128)}, f32[128,128]{1,0:T(8,128)}) custom-call(f32[640,128]{1,0:T(8,128)S(1)} %bitcast.39, f32[128,128]{1,0:T(8,128)S(1)} %get-tuple-element.47.refs_1_.refs_0_, f32[128,128]{1,0:T(8,128)S(1)} %bond_force.1.refs_2_, f32[128,128]{1,0:T(8,128)S(1)} %bitcast.48, f32[128,128]{1,0:T(8,128)S(1)} %bitcast.50), custom_call_target="tpu_custom_call" | custom-call | flops 10000000 | bytes 1000000 | tf_op jit(solution)/shard_map/coarse_out/pallas_call | solution.py:480
  67.0 0.0 copy-done.8
  67.0 0.0 copy-done
  67.0 0.0 copy-done.1
  67.0 0.1 copy-done.2
  67.1 0.3 fine_own.1
  67.3 5.3 %all-to-all-done.1 = f32[128,4,128]{2,1,0:T(4,128)S(1)} async-done(((f32[128,4,128]{2,1,0:T(4,128)}), f32[128,4,128]{2,1,0:T(4,128)S(1)}, u32[]{:S(2)}, u32[]{:S(2)}) %all-to-all-start.1) | async-done | bytes 262176 | tf_op jit(solution)/shard_map/all_to_all | solution.py:383
  72.6 1.2 %finish.1 = (f32[384,128]{1,0:T(8,128)}, f32[384,128]{1,0:T(8,128)}) custom-call(f32[512,128]{1,0:T(8,128)S(1)} %bitcast.40, f32[384,128]{1,0:T(8,128)S(1)} %get-tuple-element.61.refs_1_, f32[384,128]{1,0:T(8,128)S(1)} %get-tuple-element.62.refs_2_, bf16[96,256]{1,0:T(8,128)(2,1)S(1)} %get-tuple-element.63.refs_3_), custom_call_target="tpu_custom_call" | custom-call | flops 1000000 | bytes 1000000 | tf_op jit(solution)/shard_map/finish/pallas_call | solution.py:498
  (1 shorter events, 0.0 us)
Async XLA Ops:
  3.1 25.1 %copy-start.3 = (f32[2,2,32,128]{3,2,1,0:T(8,128)S(1)}, f32[2,2,32,128]{3,2,1,0:T(8,128)}, u32[]{:S(2)}) copy-start(f32[2,2,32,128]{3,2,1,0:T(8,128)} %param.11) | copy-start | bytes 196612
  3.1 25.1 %copy-start.4 = (f32[2,2,32,128]{3,2,1,0:T(8,128)S(1)}, f32[2,2,32,128]{3,2,1,0:T(8,128)}, u32[]{:S(2)}) copy-start(f32[2,2,32,128]{3,2,1,0:T(8,128)} %param.12) | copy-start | bytes 196612
  3.1 25.1 %copy-start.5 = (f32[2,2,32,128]{3,2,1,0:T(8,128)S(1)}, f32[2,2,32,128]{3,2,1,0:T(8,128)}, u32[]{:S(2)}) copy-start(f32[2,2,32,128]{3,2,1,0:T(8,128)} %param.10) | copy-start | bytes 196612
  3.1 25.1 %copy-start.6 = (s32[2,32,128]{2,1,0:T(8,128)S(1)}, s32[2,32,128]{2,1,0:T(8,128)}, u32[]{:S(2)}) copy-start(s32[2,32,128]{2,1,0:T(8,128)} %param.13) | copy-start | bytes 98308
  3.1 25.0 %copy-start.7 = (s32[2,32,128]{2,1,0:T(8,128)S(1)}, s32[2,32,128]{2,1,0:T(8,128)}, u32[]{:S(2)}) copy-start(s32[2,32,128]{2,1,0:T(8,128)} %param.14) | copy-start | bytes 98308
  3.1 40.0 %all-to-all-start = ((f32[128,1,640]{2,1,0:T(1,128)}), f32[128,1,640]{2,1,0:T(1,128)S(1)}, u32[]{:S(2)}, u32[]{:S(2)}) async-start(f32[128,1,640]{2,1,0:T(1,128)} %bitcast.58), calls=%async_computation | async-start | bytes 655360 | tf_op jit(solution)/shard_map/all_to_all | solution.py:383
  28.2 14.9 %collective-permute-start.2 = (f32[96,128]{1,0:T(8,128)S(1)}, f32[96,128]{1,0:T(8,128)S(1)}, u32[]{:S(2)}, u32[]{:S(2)}) collective-permute-start(f32[96,128]{1,0:T(8,128)S(1)} %get-tuple-element.43), channel_id=1, source_target_pairs={{0,1},{1,2},{2,3},{4,5},{5,6},{6,7},{8,9},{9,10},{10,11},{12,13},{... | collective-permute-start | bytes 147464 | tf_op jit(solution)/shard_map/ppermute | solution.py:449
  31.4 11.7 %collective-permute-start.3 = (f32[96,128]{1,0:T(8,128)S(1)}, f32[96,128]{1,0:T(8,128)S(1)}, u32[]{:S(2)}, u32[]{:S(2)}) collective-permute-start(f32[96,128]{1,0:T(8,128)S(1)} %get-tuple-element.44), channel_id=1, source_target_pairs={{1,0},{2,1},{3,2},{5,4},{6,5},{7,6},{9,8},{10,9},{11,10},{13,12},{... | collective-permute-start | bytes 147464 | tf_op jit(solution)/shard_map/ppermute | solution.py:449
  32.7 9.5 %collective-permute-start = (f32[48,128]{1,0:T(8,128)S(1)}, f32[48,128]{1,0:T(8,128)S(1)}, u32[]{:S(2)}, u32[]{:S(2)}) collective-permute-start(f32[48,128]{1,0:T(8,128)S(1)} %get-tuple-element.41), channel_id=1, source_target_pairs={{0,4},{4,8},{8,12},{12,16},{16,20},{20,24},{24,28},{28,32},{32,36}... | collective-permute-start | bytes 73736 | tf_op jit(solution)/shard_map/ppermute | solution.py:446
  35.5 7.7 %collective-permute-start.1 = (f32[48,128]{1,0:T(8,128)S(1)}, f32[48,128]{1,0:T(8,128)S(1)}, u32[]{:S(2)}, u32[]{:S(2)}) collective-permute-start(f32[48,128]{1,0:T(8,128)S(1)} %get-tuple-element.42), channel_id=1, source_target_pairs={{4,0},{8,4},{12,8},{16,12},{20,16},{24,20},{28,24},{32,28},{36,32}... | collective-permute-start | bytes 73736 | tf_op jit(solution)/shard_map/ppermute | solution.py:446
  44.2 28.5 %all-to-all-start.1 = ((f32[128,4,128]{2,1,0:T(4,128)}), f32[128,4,128]{2,1,0:T(4,128)S(1)}, u32[]{:S(2)}, u32[]{:S(2)}) async-start(f32[128,4,128]{2,1,0:T(4,128)} %bitcast.26), calls=%async_computation.1 | async-start | bytes 524288 | tf_op jit(solution)/shard_map/all_to_all | solution.py:383
  60.9 6.1 %copy-start.8 = (s32[96,1]{0,1:T(1,128)S(1)}, s32[96,1]{0,1:T(1,128)}, u32[]{:S(2)}) copy-start(s32[96,1]{0,1:T(1,128)} %param.18) | copy-start | bytes 1156
  65.9 1.0 %copy-start = (f32[96,2,256]{2,1,0:T(2,128)S(1)}, f32[96,2,256]{2,1,0:T(2,128)}, u32[]{:S(2)}) copy-start(f32[96,2,256]{2,1,0:T(2,128)} %param.15) | copy-start | bytes 589828
  66.0 1.0 %copy-start.1 = (f32[96,2,256]{2,1,0:T(2,128)S(1)}, f32[96,2,256]{2,1,0:T(2,128)}, u32[]{:S(2)}) copy-start(f32[96,2,256]{2,1,0:T(2,128)} %param.16) | copy-start | bytes 589828
  66.0 1.1 %copy-start.2 = (f32[96,2,256]{2,1,0:T(2,128)S(1)}, f32[96,2,256]{2,1,0:T(2,128)}, u32[]{:S(2)}) copy-start(f32[96,2,256]{2,1,0:T(2,128)} %param.17) | copy-start | bytes 589828

commit v2 on v1

--- a/solution.py
+++ b/solution.py
@@ -16,10 +16,17 @@
     return lax.broadcasted_iota(I32, shape, dim)
 
 
-def place(patch, patches):
-    if patches != 128:
-        return patch
-    return patch ^ 80
+def place(chip, chips):
+    if chips != 64:
+        return chip
+    return chip ^ 40
+
+
+def slot_of(owner, rank, patches):
+    chips = patches // 2
+    core = lax.axis_index("patch") & 1
+    group = ((owner & 1) ^ core) * 2 + rank
+    return group * chips + place(owner >> 1, chips)
 
 
 def split3(x):
@@ -30,6 +37,11 @@
     return (high, mid, low)
 
 
+def split2(x):
+    high = x.astype(BF16)
+    return (high, (x - high.astype(F32)).astype(BF16))
+
+
 def dot(a, b):
     return jnp.dot(a, b, preferred_element_type=F32)
 
@@ -67,11 +79,10 @@
 
 
 def slot_choice(owner, blocks, patches):
-    owner_row = place(owner[...], patches)
+    owner_row = owner[...]
     owner_col = to_col(owner_row, blocks)
     rank = rank_row(owner_col, owner_row, blocks)
-    slot = iota((2 * patches, blocks), 0)
-    return (owner_row == slot % patches) & (rank == slot // patches)
+    return iota((2 * patches, blocks), 0) == slot_of(owner_row, rank, patches)
 
 
 def load_all(pairs, sems):
@@ -96,10 +107,12 @@
         copy.wait()
     chosen = slot_choice(owner, blocks, patches)
     named = jnp.sum(jnp.where(chosen, anchor[...] + 1, 0), axis=1, keepdims=True).astype(F32)
-    lane = iota((patches, 128), 1)
-    send[pl.ds(NAMES, patches, stride=OUT_ROWS), :] = jnp.where(
-        lane == 0, named[:patches], jnp.where(lane == 1, named[patches:], 0.0)
-    )
+    chips = patches // 2
+    lane = iota((chips, 128), 1)
+    names = jnp.zeros((chips, 128), F32)
+    for group in range(4):
+        names = jnp.where(lane == group, named[group * chips : (group + 1) * chips], names)
+    send[pl.ds(NAMES, chips, stride=OUT_ROWS), :] = names
     onehot = chosen.astype(F32).astype(BF16)
     for copy in copies[2:]:
         copy.wait()
@@ -108,70 +121,93 @@
         parts = [fine_plane((fd, fv, fa), half, comp, blocks)[0] for half in range(2)]
         planes.append(jnp.concatenate(parts, axis=1))
     fine_new = jnp.concatenate(planes, axis=0)
-    restricted = sum(dot(part, weights) for part in split3(fine_new))
+    restricted = dot(jnp.concatenate(split2(fine_new), axis=0), weights)
+    restricted = restricted[: 2 * blocks] + restricted[2 * blocks :]
     by_block = jnp.concatenate([restricted[:blocks], restricted[blocks:]], axis=1)
-    put_slots(send, OUT_ROWS, sum(dot(onehot, part) for part in split3(by_block)), patches, cells)
-
-
-OUT_ROWS = 5
-NAMES = 4
-BACK_ROWS = 4
+    onehot = jnp.concatenate([onehot, onehot], axis=1)
+    moved = dot(onehot, jnp.concatenate(split2(by_block), axis=0))
+    put_slots(send, OUT_ROWS, moved, patches, cells)
+
+
+OUT_ROWS = 9
+NAMES = 8
+BACK_ROWS = 8
 
 
 def put_slots(ref, stride, value, patches, cells):
-    for k in range(2):
+    chips = patches // 2
+    for group in range(4):
         for comp in range(2):
-            ref[pl.ds(k * 2 + comp, patches, stride=stride), :] = value[
-                k * patches : (k + 1) * patches, comp * cells : (comp + 1) * cells
+            ref[pl.ds(group * 2 + comp, chips, stride=stride), :] = value[
+                group * chips : (group + 1) * chips, comp * cells : (comp + 1) * cells
             ]
 
 
-def get_slots(ref, stride, patches):
+def get_slots(ref, stride, patches, groups):
+    chips = patches // 2
     slots = []
-    for k in range(2):
-        rows = [pl.ds(k * 2 + comp, patches, stride=stride) for comp in range(2)]
+    for group in groups:
+        rows = [pl.ds(group * 2 + comp, chips, stride=stride) for comp in range(2)]
         slots.append(jnp.concatenate([ref[at, :] for at in rows], axis=1))
     return jnp.concatenate(slots, axis=0)
 
 
-def slot_rows(got, patches, rows):
-    names = got[pl.ds(NAMES, patches, stride=OUT_ROWS), :]
-    row = (iota((patches, rows), 1) + 1).astype(F32)
-    parts = [(names[:, k : k + 1] == row).astype(F32).astype(BF16) for k in range(2)]
+def slot_rows(got, patches, rows, groups):
+    chips = patches // 2
+    names = got[pl.ds(NAMES, chips, stride=OUT_ROWS), :]
+    row = (iota((chips, rows), 1) + 1).astype(F32)
+    parts = [(names[:, g : g + 1] == row).astype(F32).astype(BF16) for g in groups]
     return jnp.concatenate(parts, axis=0)
 
 
-def rows_kernel(patches, cells, rows, got, new, send):
-    onehot = slot_rows(got, patches, rows)
-    grid = jnp.concatenate([new[:rows, :], new[rows:, :]], axis=1)
-    put_slots(send, BACK_ROWS, sum(dot(onehot, part) for part in split3(grid)), patches, cells)
-
-
-def coarse_kernel(patches, cells, rows, got, coarse, bond, vel, acc, accel_out, velocity_out):
-    onehot = slot_rows(got, patches, rows)
-    summed = sum(dot_ta(onehot, part) for part in split3(get_slots(got, OUT_ROWS, patches)))
-    count = dot_ta(onehot, jnp.ones((2 * patches, cells), BF16))
+def rows_kernel(patches, cells, rows, got, new, other, send):
+    for side, grid in enumerate((new, other)):
+        groups = (2 * side, 2 * side + 1)
+        onehot = jnp.concatenate([slot_rows(got, patches, rows, groups)] * 3, axis=1)
+        grid = jnp.concatenate([grid[:rows, :], grid[rows : 2 * rows, :]], axis=1)
+        taken = dot(onehot, jnp.concatenate(split3(grid), axis=0))
+        chips = patches // 2
+        for n, group in enumerate(groups):
+            for comp in range(2):
+                send[pl.ds(group * 2 + comp, chips, stride=BACK_ROWS), :] = taken[
+                    n * chips : (n + 1) * chips, comp * cells : (comp + 1) * cells
+                ]
+
+
+def reaction_kernel(patches, cells, rows, got, new, other, own_out, other_out):
     lane = iota((rows, cells), 1)
+    for side, (grid, out) in enumerate(((new, own_out), (other, other_out))):
+        groups = (2 * side, 2 * side + 1)
+        onehot = slot_rows(got, patches, rows, groups)
+        summed = sum(dot_ta(onehot, x) for x in split3(get_slots(got, OUT_ROWS, patches, groups)))
+        count = dot_ta(onehot, jnp.ones((patches, cells), BF16))
+        for comp in range(2):
+            own = slice(comp * rows, (comp + 1) * rows)
+            row = grid[own, :]
+            after = jnp.where(lane == cells - 1, row, pltpu.roll(row, cells - 1, 1))
+            odd = 0.5 * (row + after)
+            before = jnp.where(lane == 0, 0.0, pltpu.roll(odd, 1, 1))
+            ending = jnp.where(lane == cells - 1, odd, 0.0)
+            folded = row + 0.5 * odd + 0.5 * (before + ending)
+            out[own, :] = summed[:, comp * cells : (comp + 1) * cells] - count * folded
+
+
+def coarse_kernel(
+    rows, coarse, bond, horizon, below, above, mine, theirs, vel, acc, accel_out, velocity_out
+):
     for comp in range(2):
         own = slice(comp * rows, (comp + 1) * rows)
-        row = coarse[own, :]
-        after = jnp.where(lane == cells - 1, row, pltpu.roll(row, cells - 1, 1))
-        odd = 0.5 * (row + after)
-        before = jnp.where(lane == 0, 0.0, pltpu.roll(odd, 1, 1))
-        ending = jnp.where(lane == cells - 1, odd, 0.0)
-        folded = row + 0.5 * odd + 0.5 * (before + ending)
-        reaction = summed[:, comp * cells : (comp + 1) * cells] - count * folded
-        accel = bond[own, :] + reaction
+        layer = layer_force(rows // 2, coarse, horizon, below, above, comp)
+        accel = bond[own, :] + layer + (mine[own, :] + theirs[own, :])
         accel_out[own, :] = accel
         velocity_out[own, :] = vel[own, :] + 0.5 * STEP * (acc[own, :] + accel)
 
 
 def fine_own_kernel(blocks, patches, fd, fv, fa, owner, accel_base, velocity_base, fine_onehot):
-    owner_row = place(owner[...], patches)
+    owner_row = owner[...]
     owner_col = to_col(owner_row, blocks)
     rank = rank_col(owner_col, owner_row, blocks)
-    slot = iota((blocks, 2 * patches), 1)
-    chosen = (owner_col == slot % patches) & (rank == slot // patches)
+    chosen = iota((blocks, 2 * patches), 1) == slot_of(owner_col, rank, patches)
     fine_onehot[...] = chosen.astype(F32).astype(BF16)
     lane = iota((blocks, 128), 1)
     for comp in range(2):
@@ -198,11 +234,11 @@
     onehot = fine_onehot[...]
     points = 2 * cells
     weights = refine_weights(iota((cells, points), 0), iota((cells, points), 1), cells)
-    refined = jnp.zeros((2 * blocks, points), F32)
-    for part in split3(get_slots(got, BACK_ROWS, patches)):
-        taken = dot(onehot, part).astype(BF16)
-        taken = jnp.concatenate([taken[:, :cells], taken[:, cells:]], axis=0)
-        refined = refined + dot(taken, weights)
+    slots = jnp.concatenate(split2(get_slots(got, BACK_ROWS, patches, range(4))), axis=1)
+    taken = dot(onehot, slots).astype(BF16)
+    taken = [taken[:, n * cells : (n + 1) * cells] for n in range(4)]
+    refined = dot(jnp.concatenate(taken, axis=0), weights)
+    refined = refined[: 2 * blocks] + refined[2 * blocks :]
     for comp in range(2):
         for half in range(2):
             at = pl.ds(half * 2 + comp, blocks, stride=4)
@@ -211,17 +247,22 @@
             velocity_out[at, :] = velocity_base[at, :] + 0.5 * STEP * added
 
 
-def prepare_kernel(inner_x, disp, vel, acc, horizon, crack, new, low, high, below, above):
+def prepare_kernel(inner_x, disp, vel, acc, horizon, crack, new, swap, edge, below, above):
     rows = 2 * inner_x
+    first = (lax.axis_index("patch") & 1) == 0
     value = disp[...] + STEP * vel[...] + (0.5 * STEP * STEP) * acc[...]
     new[...] = value
+    swap[: 2 * rows, :] = value
     fields = (value[:rows], value[rows:], horizon[...].astype(F32), crack[...].astype(F32))
     for f, field in enumerate(fields):
         for layer in range(2):
             at = (f * 2 + layer) * RADIUS
             begin, end = layer * inner_x, (layer + 1) * inner_x
-            low[at : at + RADIUS, :] = field[end - RADIUS : end]
-            high[at : at + RADIUS, :] = field[begin : begin + RADIUS]
+            head, tail = field[begin : begin + RADIUS], field[end - RADIUS : end]
+            edge[at : at + RADIUS, :] = jnp.where(first, head, tail)
+            if f >= 2:
+                at = 2 * rows + at - 4 * RADIUS
+                swap[at : at + RADIUS, :] = jnp.where(first, tail, head)
         if f < 3:
             below[f * inner_x : (f + 1) * inner_x, :] = field[inner_x:]
             above[f * inner_x : (f + 1) * inner_x, :] = field[:inner_x]
@@ -246,25 +287,41 @@
     return jnp.where(present, 2.0 / (guard * guard), 0.0)
 
 
-FIELDS = 8
+FIELDS = 4
 LEVELS = (2, 3, 4, 5, 6)
 
 
-def bond_kernel(inner_x, new, horizon, crack, low, high, below, above, out, wide, moved, there):
+def reaching(micro, level):
+    if level == 2:
+        return micro
+    return jnp.where(micro < 2.0 / (level - 0.5) ** 2, micro, 0.0)
+
+
+def bond_kernel(inner_x, new, horizon, crack, swap, edge, out, wide, moved, there):
     rows = 2 * inner_x
     cells = 128
+    first = (lax.axis_index("patch") & 1) == 0
     extent = inner_x + 2 * RADIUS
     for layer in range(2):
         begin = layer * inner_x
         for f in range(4):
             at = (f * 2 + layer) * RADIUS
-            wide[f, layer, 0:RADIUS, :] = low[at : at + RADIUS, :]
-            wide[f, layer, RADIUS + inner_x : extent, :] = high[at : at + RADIUS, :]
+            beyond = edge[at : at + RADIUS, :]
+            if f < 2:
+                grid = swap[f * rows + begin : f * rows + begin + inner_x, :]
+                head, tail = grid[:RADIUS], grid[inner_x - RADIUS :]
+            else:
+                at = 2 * rows + at - 4 * RADIUS
+                head = tail = swap[at : at + RADIUS, :]
+            wide[f, layer, 0:RADIUS, :] = jnp.where(first, beyond, tail)
+            wide[f, layer, RADIUS + inner_x : extent, :] = jnp.where(first, head, beyond)
         middle = slice(RADIUS, RADIUS + inner_x)
         wide[0, layer, middle, :] = new[begin : begin + inner_x, :]
         wide[1, layer, middle, :] = new[rows + begin : rows + begin + inner_x, :]
         wide[2, layer, middle, :] = horizon[begin : begin + inner_x, :].astype(F32)
         wide[3, layer, middle, :] = crack[begin : begin + inner_x, :].astype(F32)
+    offsets = bond_offsets(RADIUS)
+    farthest = {b: max(abs(entry[0]) for entry in offsets[b]) for b in offsets}
     for r in range(8 + 2 * RADIUS):
         fields = [
             jnp.concatenate(
@@ -272,29 +329,18 @@
             )
             for f in range(4)
         ]
-        reach = fields[2]
-        micro = micro_of(reach)
-        there[r] = (reach > 0.0).astype(F32)
-        moved[RADIUS, 0, r] = fields[0]
-        moved[RADIUS, 1, r] = fields[1]
-        moved[RADIUS, 2, r] = fields[3]
-        for n, level in enumerate(LEVELS):
-            moved[RADIUS, 3 + n, r] = jnp.where(reach >= float(level), micro, 0.0)
-
-    def shift_row(r, carry):
-        for f in range(FIELDS):
-            field = moved[RADIUS, f, r]
-            for along_y in range(-RADIUS, RADIUS + 1):
-                if along_y != 0:
-                    moved[RADIUS + along_y, f, r] = pltpu.roll(field, (-along_y) % cells, 1)
-        return carry
-
-    lax.fori_loop(0, 8 + 2 * RADIUS, shift_row, 0)
+        there[r] = (fields[2] > 0.0).astype(F32)
+        fields = (fields[0], fields[1], fields[3], micro_of(fields[2]))
+        for along_y in range(-RADIUS, RADIUS + 1):
+            if RADIUS - farthest[along_y] <= r < 8 + RADIUS + farthest[along_y]:
+                for f, field in enumerate(fields):
+                    shifted = pltpu.roll(field, -along_y % cells, 1) if along_y else field
+                    moved[RADIUS + along_y, f, r] = shifted
     lane = iota((8, cells), 1)
-    offsets = bond_offsets(RADIUS)
 
     def force_row(i, carry):
         own = [moved[RADIUS, f, i + RADIUS] for f in range(FIELDS)]
+        own_reaching = {level: reaching(own[3], level) for level in LEVELS}
         force_x = jnp.zeros((8, cells), F32)
         force_y = jnp.zeros((8, cells), F32)
         for along_y in range(-RADIUS, RADIUS + 1):
@@ -304,7 +350,7 @@
                 r = i + (RADIUS + along_x)
                 at = RADIUS + along_y
                 scale = 1.0 / float(square) ** 1.5
-                weight = (own[1 + level] + moved[at, 1 + level, r]) * (
+                weight = (own_reaching[level] + reaching(moved[at, 3, r], level)) * (
                     there[r] - own[2] * moved[at, 2, r]
                 )
                 stretch = 0.0
@@ -327,28 +373,31 @@
         return carry
 
     lax.fori_loop(0, 8, force_row, 0)
-    reach = horizon[...].astype(F32)
-    micro = micro_of(reach)
-    for comp in range(2):
-        own = new[comp * rows : (comp + 1) * rows, :]
-        force = jnp.zeros((rows, cells), F32)
-        for side in range(2):
-            far = (below, above)[side]
-
-            def beside(mine, f):
-                outer = far[f * inner_x : (f + 1) * inner_x, :]
-                if side == 0:
-                    return jnp.concatenate([outer, mine[:inner_x]], axis=0)
-                return jnp.concatenate([mine[inner_x:], outer], axis=0)
-
-            reach_j = beside(reach, 2)
-            factor = jnp.where(reach_j > 0.0, micro + micro_of(reach_j), 0.0)
-            force = force + factor * (beside(own, comp) - own)
-        out[comp * rows : (comp + 1) * rows, :] = force
     for comp in range(2):
         for i in range(8):
             at = pl.ds(comp * rows + i, 8, stride=8)
-            out[at, :] = out[at, :] + wide[comp, 0, 8 * i : 8 * i + 8, :]
+            out[at, :] = wide[comp, 0, 8 * i : 8 * i + 8, :]
+
+
+def layer_force(inner_x, new, horizon, below, above, comp):
+    rows = 2 * inner_x
+    reach = horizon[...].astype(F32)
+    micro = micro_of(reach)
+    own = new[comp * rows : (comp + 1) * rows, :]
+    force = jnp.zeros_like(own)
+    for side in range(2):
+        far = (below, above)[side]
+
+        def beside(mine, f):
+            outer = far[f * inner_x : (f + 1) * inner_x, :]
+            if side == 0:
+                return jnp.concatenate([outer, mine[:inner_x]], axis=0)
+            return jnp.concatenate([mine[inner_x:], outer], axis=0)
+
+        reach_j = beside(reach, 2)
+        factor = jnp.where(reach_j > 0.0, micro + micro_of(reach_j), 0.0)
+        force = force + factor * (beside(own, comp) - own)
+    return force
 
 
 def shape(*dims, dtype=F32):
@@ -379,10 +428,16 @@
 
 
 def exchange(x, patches):
-    order = sorted(range(patches), key=lambda patch: place(patch, patches))
+    chips = patches // 2
+    order = sorted(range(chips), key=lambda chip: place(chip, chips))
+    groups = [[2 * chip + core for chip in order] for core in range(2)]
     return lax.all_to_all(
-        x, "patch", split_axis=0, concat_axis=0, tiled=True, axis_index_groups=[order]
-    )
+        x, "patch", split_axis=0, concat_axis=0, tiled=True, axis_index_groups=groups
+    )
+
+
+def to_other_core(x, patches):
+    return lax.ppermute(x, "patch", [(i, i ^ 1) for i in range(patches)])
 
 
 def body(
@@ -402,6 +457,7 @@
     blocks = fine_disp.shape[0]
     patches = lax.axis_size("patch")
     slabs = lax.axis_size("slab")
+    chips = patches // 2
     fine = [fine_view(x) for x in (fine_disp, fine_vel, fine_acc)]
     owner = fine_owner.reshape(1, blocks)
     anchor = fine_anchor.reshape(1, blocks)
@@ -411,7 +467,7 @@
 
     send = call(
         lambda *refs: pack_kernel(blocks, patches, cells, *refs),
-        shape(OUT_ROWS * patches, cells),
+        shape(OUT_ROWS * chips, cells),
         "pack_fine",
         2 * 10**6,
         10**6,
@@ -422,17 +478,16 @@
             pltpu.SemaphoreType.DMA((5,)),
         ),
         in_specs=[pl.BlockSpec(memory_space=pltpu.HBM)] * 5,
-        vmem=60 * 2**20,
-    )(owner, anchor, *fine)
+    )(*[pltpu.with_memory_space_constraint(x, pltpu.HBM) for x in (owner, anchor, *fine)])
     send, grid, reach, crack = lax.optimization_barrier((send, grid, reach, crack))
-    got = exchange(send.reshape(patches, 1, OUT_ROWS * cells), patches)
-    got = got.reshape(OUT_ROWS * patches, cells)
-
-    new, low, high, below, above = call(
+    got = exchange(send.reshape(chips, 1, OUT_ROWS * cells), patches)
+    got = got.reshape(OUT_ROWS * chips, cells)
+
+    new, swap, edge, below, above = call(
         lambda *refs: prepare_kernel(inner_x, *refs),
         (
             shape(2 * rows, cells),
-            shape(8 * RADIUS, cells),
+            shape(2 * rows + 4 * RADIUS, cells),
             shape(8 * RADIUS, cells),
             shape(3 * inner_x, cells),
             shape(3 * inner_x, cells),
@@ -441,26 +496,25 @@
         10**6,
         10**6,
     )(*grid, reach, crack)
-    up = [(i, i + 1) for i in range(patches - 1)]
-    down = [(i + 1, i) for i in range(patches - 1)]
-    low, high = lax.ppermute(low, "patch", up), lax.ppermute(high, "patch", down)
+    swap = to_other_core(swap, patches)
+    pairs = [(i, i + 1) for i in range(1, patches - 1, 2)]
+    edge = lax.ppermute(edge, "patch", pairs + [(b, a) for a, b in pairs])
     up = [(i, i + 1) for i in range(slabs - 1)]
     down = [(i + 1, i) for i in range(slabs - 1)]
     below, above = lax.ppermute(below, "slab", up), lax.ppermute(above, "slab", down)
-
-    got, low, high, below, above = lax.optimization_barrier((got, low, high, below, above))
+    got, edge, below, above = lax.optimization_barrier((got, edge, below, above))
     send = call(
         lambda *refs: rows_kernel(patches, cells, rows, *refs),
-        shape(BACK_ROWS * patches, cells),
+        shape(BACK_ROWS * chips, cells),
         "take_rows",
         2 * 10**6,
         10**6,
-    )(got, new)
+    )(got, new, swap)
     send, new, reach, crack, fine, owner = lax.optimization_barrier(
         (send, new, reach, crack, fine, owner)
     )
-    returned = exchange(send.reshape(patches, BACK_ROWS, cells), patches)
-    returned = returned.reshape(BACK_ROWS * patches, cells)
+    returned = exchange(send.reshape(chips, BACK_ROWS, cells), patches)
+    returned = returned.reshape(BACK_ROWS * chips, cells)
 
     span = 8 + 2 * RADIUS
     bond = call(
@@ -475,15 +529,23 @@
             pltpu.VMEM((span, 8, cells), F32),
         ),
         vmem=32 * 2**20,
-    )(new, reach, crack, low, high, below, above)
-
+    )(new, reach, crack, swap, edge)
+
+    mine, theirs = call(
+        lambda *refs: reaction_kernel(patches, cells, rows, *refs),
+        (shape(2 * rows, cells), shape(2 * rows, cells)),
+        "reaction",
+        10**7,
+        10**6,
+    )(got, new, swap)
+    theirs = to_other_core(theirs, patches)
     coarse_accel, coarse_velocity = call(
-        lambda *refs: coarse_kernel(patches, cells, rows, *refs),
+        lambda *refs: coarse_kernel(rows, *refs),
         (shape(2 * rows, cells), shape(2 * rows, cells)),
         "coarse_out",
         10**7,
         10**6,
-    )(got, new, bond, grid[1], grid[2])
+    )(new, bond, reach, below, above, mine, theirs, grid[1], grid[2])
     fine_base = call(
         lambda *refs: fine_own_kernel(blocks, patches, *refs),
         (

time: 74.3 us -> 68.9 us (0.927)
  waiting for transfers between devices: 11 us -> 8.07 us
  Pallas kernels: 11 us -> 8.44 us
    ppermute x2 -> x3, starting transfers between devices: 4.65 us -> 8.79 us  [the longest x2 6.42 us: to_other_core(): return lax.ppermute(x, 'patch', [(i, i ^ 1) for i in range(patches)])]
    all_to_all x2, starting transfers between devices: 41.7 us -> 37.8 us  [exchange(): lax.all_to_all(x, 'patch', split_axis=0, concat_axis=0, tiled=True, axis_...]
    pallas_call x1, Pallas kernels: 5.07 us -> 2.65 us  [body(): call(lambda *refs: bond_kernel(inner_x, *refs), shape(2 * rows, cells), '...]
    ppermute x2 -> x3, waiting for transfers between devices: 5.75 us -> 3.95 us  [the longest x1 3.95 us: body(): edge = lax.ppermute(edge, 'patch', pairs + [(b, a) for a, b in pairs])]
    all_to_all x2, waiting for transfers between devices: 5.28 us -> 4.12 us  [exchange(): lax.all_to_all(x, 'patch', split_axis=0, concat_axis=0, tiled=True, axis_...]
  transfers between devices with their start and end apart: 6 -> 7, of which waited for: 3 -> 2; matrix products, arithmetic and copies ran while one was open for 0% -> 0% of each run, Pallas kernels for 9% -> 6%
where the time goes in v2:
time: 68.9 us; the launch traced here: 68.5 us
  starting transfers between devices  51 us (74%)
  Pallas kernels  8.44 us (12%)
  waiting for transfers between devices  8.07 us (12%)
  between operations  0.88 us (1%)
    all_to_all x2, starting transfers between devices, exchange(): lax.all_to_all(x, 'patch', split_axis=0, concat_axis=0, tiled=True, axis_...  37.8 us
    ppermute x2, starting transfers between devices, to_other_core(): return lax.ppermute(x, 'patch', [(i, i ^ 1) for i in range(patches)])  6.42 us
    all_to_all x2, waiting for transfers between devices, exchange(): lax.all_to_all(x, 'patch', split_axis=0, concat_axis=0, tiled=True, axis_...  4.12 us
    ppermute x1, waiting for transfers between devices, body(): edge = lax.ppermute(edge, 'patch', pairs + [(b, a) for a, b in pairs])  3.95 us
    ppermute x1, starting transfers between devices, body(): lax.ppermute(below, 'slab', up)  3.2 us
    pallas_call x1, Pallas kernels, body(): call(lambda *refs: bond_kernel(inner_x, *refs), shape(2 * rows, cells), '...  2.65 us
    ppermute x1, starting transfers between devices, body(): edge = lax.ppermute(edge, 'patch', pairs + [(b, a) for a, b in pairs])  2.38 us
    pallas_call x1, Pallas kernels, body(): call(lambda *refs: pack_kernel(blocks, patches, cells, *refs), shape(OUT_...  2.36 us
  transfers between devices with their start and end apart: 7, of which 2 were waited for; matrix products, arithmetic and copies ran while one was open for 0% of the time, Pallas kernels for 6%

profile of v2, /device:TPU:1, one launch (start us, length us, event | category | flops | bytes accessed | tf_op | source)
XLA Modules:
  0.0 68.5 jit_solution(8992855510186182759)
XLA Ops:
  0.6 2.4 %pack_fine.1 = f32[576,128]{1,0:T(8,128)} custom-call(s32[1,96]{1,0:T(1,128)} %bitcast.57, s32[1,96]{1,0:T(1,128)} %bitcast.59, f32[384,128]{1,0:T(8,128)} %bitcast.41, f32[384,128]{1,0:T(8,128)} %bitcast.43, f32[384,128]{1,0:T(8,128)} %bitcast.45), custom_call_target="tpu_custom_call" | custom-call | flops 2000000 | bytes 1000000 | tf_op jit(solution)/shard_map/pack_fine/pallas_call | solution.py:468
  3.0 0.0 copy-start.3
  3.0 0.0 copy-start.4
  3.0 0.0 copy-start.5
  3.0 0.0 copy-start.6
  3.0 0.0 copy-start.7
  3.1 23.1 %all-to-all-start = ((f32[64,1,1152]{2,1,0:T(1,128)}), f32[64,1,1152]{2,1,0:T(1,128)S(1)}, u32[]{:S(2)}, u32[]{:S(2)}) async-start(f32[64,1,1152]{2,1,0:T(1,128)} %bitcast.16), calls=%async_computation | async-start | bytes 589824 | tf_op jit(solution)/shard_map/all_to_all | solution.py:434
  26.1 0.0 copy-done.3
  26.1 0.0 copy-done.4
  26.1 0.0 copy-done.5
  26.1 0.0 copy-done.6
  26.2 0.0 copy-done.7
  26.2 3.1 %collective-permute-start.3 = (f32[152,128]{1,0:T(8,128)S(1)}, f32[152,128]{1,0:T(8,128)S(1)}, u32[]{:S(2)}, u32[]{:S(2)}) collective-permute-start(f32[152,128]{1,0:T(8,128)S(1)} %get-tuple-element.47), channel_id=1, source_target_pairs={{0,4},{4,0},{8,12},{12,8},{16,20},{20,16},{24,28},{28,24},{32,36},... | collective-permute-start | bytes 233480 | tf_op jit(solution)/shard_map/ppermute | solution.py:440
  29.4 3.2 %collective-permute-start.1 = (f32[96,128]{1,0:T(8,128)S(1)}, f32[96,128]{1,0:T(8,128)S(1)}, u32[]{:S(2)}, u32[]{:S(2)}) collective-permute-start(f32[96,128]{1,0:T(8,128)S(1)} %get-tuple-element.43), channel_id=1, source_target_pairs={{0,1},{1,2},{2,3},{4,5},{5,6},{6,7},{8,9},{9,10},{10,11},{12,13},{... | collective-permute-start | bytes 147464 | tf_op jit(solution)/shard_map/ppermute | solution.py:504
  32.6 1.3 %collective-permute-start.2 = (f32[96,128]{1,0:T(8,128)S(1)}, f32[96,128]{1,0:T(8,128)S(1)}, u32[]{:S(2)}, u32[]{:S(2)}) collective-permute-start(f32[96,128]{1,0:T(8,128)S(1)} %get-tuple-element.44), channel_id=1, source_target_pairs={{1,0},{2,1},{3,2},{5,4},{6,5},{7,6},{9,8},{10,9},{11,10},{13,12},{... | collective-permute-start | bytes 147464 | tf_op jit(solution)/shard_map/ppermute | solution.py:504
  33.9 2.4 %collective-permute-start = (f32[48,128]{1,0:T(8,128)S(1)}, f32[48,128]{1,0:T(8,128)S(1)}, u32[]{:S(2)}, u32[]{:S(2)}) collective-permute-start(f32[48,128]{1,0:T(8,128)S(1)} %get-tuple-element.42), channel_id=1, source_target_pairs={{4,8},{12,16},{20,24},{28,32},{36,40},{44,48},{52,56},{60,64},{68,... | collective-permute-start | bytes 73736 | tf_op jit(solution)/shard_map/ppermute | solution.py:501
  36.2 3.9 %collective-permute-done.refs_4_ = f32[48,128]{1,0:T(8,128)S(1)} collective-permute-done((f32[48,128]{1,0:T(8,128)S(1)}, f32[48,128]{1,0:T(8,128)S(1)}, u32[]{:S(2)}, u32[]{:S(2)}) %collective-permute-start) | collective-permute-done | bytes 24608 | tf_op jit(solution)/shard_map/ppermute | solution.py:501
  40.2 0.0 collective-permute-done.1.refs_3_
  40.2 0.0 collective-permute-done.2.refs_4_
  40.2 0.0 all-to-all-done
  40.2 0.0 collective-permute-done.3.refs_2_.refs_3_
  40.2 1.0 %take_rows.1 = f32[512,128]{1,0:T(8,128)} custom-call(f32[576,128]{1,0:T(8,128)S(1)} %bitcast.38, f32[128,128]{1,0:T(8,128)S(1)} %get-tuple-element.48.refs_1_.refs_0_, f32[152,128]{1,0:T(8,128)S(1)} %collective-permute-done.3.refs_2_.refs_3_), custom_call_target="tpu_custom_call" | custom-call | flops 2000000 | bytes 1000000 | tf_op jit(solution)/shard_map/take_rows/pallas_call | solution.py:506
  41.2 0.0 copy-start.2
  41.2 14.7 %all-to-all-start.1 = ((f32[64,8,128]{2,1,0:T(8,128)}), f32[64,8,128]{2,1,0:T(8,128)S(1)}, u32[]{:S(2)}, u32[]{:S(2)}) async-start(f32[64,8,128]{2,1,0:T(8,128)} %bitcast.20), calls=%async_computation.1 | async-start | bytes 524288 | tf_op jit(solution)/shard_map/all_to_all | solution.py:434
  55.9 0.0 copy-start
  55.9 0.0 copy-start.1
  56.0 0.3 reaction.1
  56.3 0.0 copy-start.8
  56.3 3.3 %collective-permute-start.4 = (f32[128,128]{1,0:T(8,128)S(1)}, f32[128,128]{1,0:T(8,128)S(1)}, u32[]{:S(2)}, u32[]{:S(2)}) collective-permute-start(f32[128,128]{1,0:T(8,128)S(1)} %get-tuple-element.55), channel_id=1, source_target_pairs={{0,4},{4,0},{8,12},{12,8},{16,20},{20,16},{24,28},{28,24},{32,36},... | collective-permute-start | bytes 196616 | tf_op jit(solution)/shard_map/ppermute | solution.py:440
  59.6 0.0 copy-done.2
  59.6 0.0 copy-done
  59.6 0.0 copy-done.1
  59.6 0.0 copy-done.8
  59.6 0.3 fine_own.1
  59.9 2.6 %bond_force.1.refs_1_ = f32[128,128]{1,0:T(8,128)S(1)} custom-call(f32[128,128]{1,0:T(8,128)S(1)} %get-tuple-element.48.refs_1_.refs_0_, s32[64,128]{1,0:T(8,128)S(1)} %bitcast.52, s32[64,128]{1,0:T(8,128)S(1)} %bitcast.56, f32[152,128]{1,0:T(8,128)S(1)} %collective-permute-done.3.refs_2_.refs_3_, f32[48,128]{1,0:T(8,128)S(1)} %collective-permute-done.refs_4_), custom_call_target="tpu_custom_call" | custom-call | flops 1000000000 | bytes 10000000 | tf_op jit(solution)/shard_map/bond_force/pallas_call | solution.py:520
  62.6 0.0 collective-permute-done.4.refs_6_
  62.6 0.7 %coarse_out.1 = (f32[128,128]{1,0:T(8,128)}, f32[128,128]{1,0:T(8,128)}) custom-call(f32[128,128]{1,0:T(8,128)S(1)} %get-tuple-element.48.refs_1_.refs_0_, f32[128,128]{1,0:T(8,128)S(1)} %bond_force.1.refs_1_, s32[64,128]{1,0:T(8,128)S(1)} %bitcast.53, f32[96,128]{1,0:T(8,128)S(1)} %collective-permute-done.1.refs_3_, ...), custom_call_target="tpu_custom_call" | custom-call | flops 10000000 | bytes 1000000 | tf_op jit(solution)/shard_map/coarse_out/pallas_call | solution.py:542
  63.3 4.1 %all-to-all-done.1 = f32[64,8,128]{2,1,0:T(8,128)S(1)} async-done(((f32[64,8,128]{2,1,0:T(8,128)}), f32[64,8,128]{2,1,0:T(8,128)S(1)}, u32[]{:S(2)}, u32[]{:S(2)}) %all-to-all-start.1) | async-done | bytes 262176 | tf_op jit(solution)/shard_map/all_to_all | solution.py:434
  67.4 1.1 %finish.1 = (f32[384,128]{1,0:T(8,128)}, f32[384,128]{1,0:T(8,128)}) custom-call(f32[512,128]{1,0:T(8,128)S(1)} %bitcast.40, f32[384,128]{1,0:T(8,128)S(1)} %get-tuple-element.63.refs_1_, f32[384,128]{1,0:T(8,128)S(1)} %get-tuple-element.64.refs_2_, bf16[96,256]{1,0:T(8,128)(2,1)S(1)} %get-tuple-element.65.refs_3_), custom_call_target="tpu_custom_call" | custom-call | flops 1000000 | bytes 1000000 | tf_op jit(solution)/shard_map/finish/pallas_call | solution.py:560
  (1 shorter events, 0.0 us)
Async XLA Ops:
  3.0 23.1 %copy-start.3 = (f32[2,2,32,128]{3,2,1,0:T(8,128)S(1)}, f32[2,2,32,128]{3,2,1,0:T(8,128)}, u32[]{:S(2)}) copy-start(f32[2,2,32,128]{3,2,1,0:T(8,128)} %param.11) | copy-start | bytes 196612
  3.0 23.1 %copy-start.4 = (f32[2,2,32,128]{3,2,1,0:T(8,128)S(1)}, f32[2,2,32,128]{3,2,1,0:T(8,128)}, u32[]{:S(2)}) copy-start(f32[2,2,32,128]{3,2,1,0:T(8,128)} %param.12) | copy-start | bytes 196612
  3.0 23.1 %copy-start.5 = (s32[2,32,128]{2,1,0:T(8,128)S(1)}, s32[2,32,128]{2,1,0:T(8,128)}, u32[]{:S(2)}) copy-start(s32[2,32,128]{2,1,0:T(8,128)} %param.13) | copy-start | bytes 98308
  3.0 23.1 %copy-start.6 = (f32[2,2,32,128]{3,2,1,0:T(8,128)S(1)}, f32[2,2,32,128]{3,2,1,0:T(8,128)}, u32[]{:S(2)}) copy-start(f32[2,2,32,128]{3,2,1,0:T(8,128)} %param.10) | copy-start | bytes 196612
  3.0 23.1 %copy-start.7 = (s32[2,32,128]{2,1,0:T(8,128)S(1)}, s32[2,32,128]{2,1,0:T(8,128)}, u32[]{:S(2)}) copy-start(s32[2,32,128]{2,1,0:T(8,128)} %param.14) | copy-start | bytes 98308
  3.1 37.1 %all-to-all-start = ((f32[64,1,1152]{2,1,0:T(1,128)}), f32[64,1,1152]{2,1,0:T(1,128)S(1)}, u32[]{:S(2)}, u32[]{:S(2)}) async-start(f32[64,1,1152]{2,1,0:T(1,128)} %bitcast.16), calls=%async_computation | async-start | bytes 589824 | tf_op jit(solution)/shard_map/all_to_all | solution.py:434
  26.2 14.0 %collective-permute-start.3 = (f32[152,128]{1,0:T(8,128)S(1)}, f32[152,128]{1,0:T(8,128)S(1)}, u32[]{:S(2)}, u32[]{:S(2)}) collective-permute-start(f32[152,128]{1,0:T(8,128)S(1)} %get-tuple-element.47), channel_id=1, source_target_pairs={{0,4},{4,0},{8,12},{12,8},{16,20},{20,16},{24,28},{28,24},{32,36},... | collective-permute-start | bytes 233480 | tf_op jit(solution)/shard_map/ppermute | solution.py:440
  29.4 10.8 %collective-permute-start.1 = (f32[96,128]{1,0:T(8,128)S(1)}, f32[96,128]{1,0:T(8,128)S(1)}, u32[]{:S(2)}, u32[]{:S(2)}) collective-permute-start(f32[96,128]{1,0:T(8,128)S(1)} %get-tuple-element.43), channel_id=1, source_target_pairs={{0,1},{1,2},{2,3},{4,5},{5,6},{6,7},{8,9},{9,10},{10,11},{12,13},{... | collective-permute-start | bytes 147464 | tf_op jit(solution)/shard_map/ppermute | solution.py:504
  32.6 7.6 %collective-permute-start.2 = (f32[96,128]{1,0:T(8,128)S(1)}, f32[96,128]{1,0:T(8,128)S(1)}, u32[]{:S(2)}, u32[]{:S(2)}) collective-permute-start(f32[96,128]{1,0:T(8,128)S(1)} %get-tuple-element.44), channel_id=1, source_target_pairs={{1,0},{2,1},{3,2},{5,4},{6,5},{7,6},{9,8},{10,9},{11,10},{13,12},{... | collective-permute-start | bytes 147464 | tf_op jit(solution)/shard_map/ppermute | solution.py:504
  33.9 6.3 %collective-permute-start = (f32[48,128]{1,0:T(8,128)S(1)}, f32[48,128]{1,0:T(8,128)S(1)}, u32[]{:S(2)}, u32[]{:S(2)}) collective-permute-start(f32[48,128]{1,0:T(8,128)S(1)} %get-tuple-element.42), channel_id=1, source_target_pairs={{4,8},{12,16},{20,24},{28,32},{36,40},{44,48},{52,56},{60,64},{68,... | collective-permute-start | bytes 73736 | tf_op jit(solution)/shard_map/ppermute | solution.py:501
  41.2 18.4 %copy-start.2 = (f32[96,2,256]{2,1,0:T(2,128)S(1)}, f32[96,2,256]{2,1,0:T(2,128)}, u32[]{:S(2)}) copy-start(f32[96,2,256]{2,1,0:T(2,128)} %param.17) | copy-start | bytes 589828
  41.2 26.2 %all-to-all-start.1 = ((f32[64,8,128]{2,1,0:T(8,128)}), f32[64,8,128]{2,1,0:T(8,128)S(1)}, u32[]{:S(2)}, u32[]{:S(2)}) async-start(f32[64,8,128]{2,1,0:T(8,128)} %bitcast.20), calls=%async_computation.1 | async-start | bytes 524288 | tf_op jit(solution)/shard_map/all_to_all | solution.py:434
  55.9 3.7 %copy-start = (f32[96,2,256]{2,1,0:T(2,128)S(1)}, f32[96,2,256]{2,1,0:T(2,128)}, u32[]{:S(2)}) copy-start(f32[96,2,256]{2,1,0:T(2,128)} %param.15) | copy-start | bytes 589828
  55.9 3.7 %copy-start.1 = (f32[96,2,256]{2,1,0:T(2,128)S(1)}, f32[96,2,256]{2,1,0:T(2,128)}, u32[]{:S(2)}) copy-start(f32[96,2,256]{2,1,0:T(2,128)} %param.16) | copy-start | bytes 589828
  56.3 3.3 %copy-start.8 = (s32[96,1]{0,1:T(1,128)S(1)}, s32[96,1]{0,1:T(1,128)}, u32[]{:S(2)}) copy-start(s32[96,1]{0,1:T(1,128)} %param.18) | copy-start | bytes 1156
  56.3 6.3 %collective-permute-start.4 = (f32[128,128]{1,0:T(8,128)S(1)}, f32[128,128]{1,0:T(8,128)S(1)}, u32[]{:S(2)}, u32[]{:S(2)}) collective-permute-start(f32[128,128]{1,0:T(8,128)S(1)} %get-tuple-element.55), channel_id=1, source_target_pairs={{0,4},{4,0},{8,12},{12,8},{16,20},{20,16},{24,28},{28,24},{32,36},... | collective-permute-start | bytes 196616 | tf_op jit(solution)/shard_map/ppermute | solution.py:440

commit v3 on v2

--- a/solution.py
+++ b/solution.py
@@ -163,9 +163,9 @@
 def rows_kernel(patches, cells, rows, got, new, other, send):
     for side, grid in enumerate((new, other)):
         groups = (2 * side, 2 * side + 1)
-        onehot = jnp.concatenate([slot_rows(got, patches, rows, groups)] * 3, axis=1)
+        onehot = jnp.concatenate([slot_rows(got, patches, rows, groups)] * 2, axis=1)
         grid = jnp.concatenate([grid[:rows, :], grid[rows : 2 * rows, :]], axis=1)
-        taken = dot(onehot, jnp.concatenate(split3(grid), axis=0))
+        taken = dot(onehot, jnp.concatenate(split2(grid), axis=0))
         chips = patches // 2
         for n, group in enumerate(groups):
             for comp in range(2):
@@ -203,7 +203,11 @@
         velocity_out[own, :] = vel[own, :] + 0.5 * STEP * (acc[own, :] + accel)
 
 
-def fine_own_kernel(blocks, patches, fd, fv, fa, owner, accel_base, velocity_base, fine_onehot):
+def fine_own_kernel(
+    blocks, patches, cells, fd, fv, fa, owner, accel_base, velocity_base, fine_onehot, refine
+):
+    points = 2 * cells
+    refine[...] = refine_weights(iota((cells, points), 0), iota((cells, points), 1), cells)
     owner_row = owner[...]
     owner_col = to_col(owner_row, blocks)
     rank = rank_col(owner_col, owner_row, blocks)
@@ -229,11 +233,10 @@
 
 
 def finish_kernel(
-    blocks, patches, cells, got, accel_base, velocity_base, fine_onehot, accel_out, velocity_out
+    blocks, patches, cells, got, accel_base, velocity_base, fine_onehot, refine, accel_out, velocity_out
 ):
     onehot = fine_onehot[...]
-    points = 2 * cells
-    weights = refine_weights(iota((cells, points), 0), iota((cells, points), 1), cells)
+    weights = refine[...]
     slots = jnp.concatenate(split2(get_slots(got, BACK_ROWS, patches, range(4))), axis=1)
     taken = dot(onehot, slots).astype(BF16)
     taken = [taken[:, n * cells : (n + 1) * cells] for n in range(4)]
@@ -547,11 +550,12 @@
         10**6,
     )(new, bond, reach, below, above, mine, theirs, grid[1], grid[2])
     fine_base = call(
-        lambda *refs: fine_own_kernel(blocks, patches, *refs),
+        lambda *refs: fine_own_kernel(blocks, patches, cells, *refs),
         (
             shape(4 * blocks, 128),
             shape(4 * blocks, 128),
             shape(blocks, 2 * patches, dtype=BF16),
+            shape(cells, 2 * cells, dtype=BF16),
         ),
         "fine_own",
         10**7,

time: 68.9 us -> 68.9 us (level)
  no operation moved by 1% of the time
where the time goes in v3:
time: 68.9 us; the launch traced here: 68.5 us
  starting transfers between devices  51 us (74%)
  Pallas kernels  8.46 us (12%)
  waiting for transfers between devices  8.06 us (12%)
  between operations  0.88 us (1%)
    all_to_all x2, starting transfers between devices, exchange(): lax.all_to_all(x, 'patch', split_axis=0, concat_axis=0, tiled=True, axis_...  37.8 us
    ppermute x2, starting transfers between devices, to_other_core(): return lax.ppermute(x, 'patch', [(i, i ^ 1) for i in range(patches)])  6.42 us
    all_to_all x2, waiting for transfers between devices, exchange(): lax.all_to_all(x, 'patch', split_axis=0, concat_axis=0, tiled=True, axis_...  4.1 us
    ppermute x1, waiting for transfers between devices, body(): edge = lax.ppermute(edge, 'patch', pairs + [(b, a) for a, b in pairs])  3.95 us
    ppermute x1, starting transfers between devices, body(): lax.ppermute(below, 'slab', up)  3.2 us
    pallas_call x1, Pallas kernels, body(): call(lambda *refs: bond_kernel(inner_x, *refs), shape(2 * rows, cells), '...  2.65 us
    ppermute x1, starting transfers between devices, body(): edge = lax.ppermute(edge, 'patch', pairs + [(b, a) for a, b in pairs])  2.38 us
    pallas_call x1, Pallas kernels, body(): call(lambda *refs: pack_kernel(blocks, patches, cells, *refs), shape(OUT_...  2.36 us
  transfers between devices with their start and end apart: 7, of which 2 were waited for; matrix products, arithmetic and copies ran while one was open for 0% of the time, Pallas kernels for 6%

profile of v3, /device:TPU:1, one launch (start us, length us, event | category | flops | bytes accessed | tf_op | source)
XLA Modules:
  0.0 68.5 jit_solution(10198719347714634636)
XLA Ops:
  0.6 2.4 %pack_fine.1 = f32[576,128]{1,0:T(8,128)} custom-call(s32[1,96]{1,0:T(1,128)} %bitcast.57, s32[1,96]{1,0:T(1,128)} %bitcast.59, f32[384,128]{1,0:T(8,128)} %bitcast.41, f32[384,128]{1,0:T(8,128)} %bitcast.43, f32[384,128]{1,0:T(8,128)} %bitcast.45), custom_call_target="tpu_custom_call" | custom-call | flops 2000000 | bytes 1000000 | tf_op jit(solution)/shard_map/pack_fine/pallas_call | solution.py:471
  3.0 0.0 copy-start.3
  3.0 0.0 copy-start.4
  3.0 0.0 copy-start.5
  3.0 0.0 copy-start.6
  3.0 0.0 copy-start.7
  3.1 23.1 %all-to-all-start = ((f32[64,1,1152]{2,1,0:T(1,128)}), f32[64,1,1152]{2,1,0:T(1,128)S(1)}, u32[]{:S(2)}, u32[]{:S(2)}) async-start(f32[64,1,1152]{2,1,0:T(1,128)} %bitcast.16), calls=%async_computation | async-start | bytes 589824 | tf_op jit(solution)/shard_map/all_to_all | solution.py:437
  26.1 0.0 copy-done.3
  26.1 0.0 copy-done.4
  26.1 0.0 copy-done.5
  26.1 0.0 copy-done.6
  26.2 0.0 copy-done.7
  26.2 3.1 %collective-permute-start.3 = (f32[152,128]{1,0:T(8,128)S(1)}, f32[152,128]{1,0:T(8,128)S(1)}, u32[]{:S(2)}, u32[]{:S(2)}) collective-permute-start(f32[152,128]{1,0:T(8,128)S(1)} %get-tuple-element.48), channel_id=1, source_target_pairs={{0,4},{4,0},{8,12},{12,8},{16,20},{20,16},{24,28},{28,24},{32,36},... | collective-permute-start | bytes 233480 | tf_op jit(solution)/shard_map/ppermute | solution.py:443
  29.4 3.2 %collective-permute-start.1 = (f32[96,128]{1,0:T(8,128)S(1)}, f32[96,128]{1,0:T(8,128)S(1)}, u32[]{:S(2)}, u32[]{:S(2)}) collective-permute-start(f32[96,128]{1,0:T(8,128)S(1)} %get-tuple-element.44), channel_id=1, source_target_pairs={{0,1},{1,2},{2,3},{4,5},{5,6},{6,7},{8,9},{9,10},{10,11},{12,13},{... | collective-permute-start | bytes 147464 | tf_op jit(solution)/shard_map/ppermute | solution.py:507
  32.6 1.3 %collective-permute-start.2 = (f32[96,128]{1,0:T(8,128)S(1)}, f32[96,128]{1,0:T(8,128)S(1)}, u32[]{:S(2)}, u32[]{:S(2)}) collective-permute-start(f32[96,128]{1,0:T(8,128)S(1)} %get-tuple-element.45), channel_id=1, source_target_pairs={{1,0},{2,1},{3,2},{5,4},{6,5},{7,6},{9,8},{10,9},{11,10},{13,12},{... | collective-permute-start | bytes 147464 | tf_op jit(solution)/shard_map/ppermute | solution.py:507
  33.9 2.4 %collective-permute-start = (f32[48,128]{1,0:T(8,128)S(1)}, f32[48,128]{1,0:T(8,128)S(1)}, u32[]{:S(2)}, u32[]{:S(2)}) collective-permute-start(f32[48,128]{1,0:T(8,128)S(1)} %get-tuple-element.43), channel_id=1, source_target_pairs={{4,8},{12,16},{20,24},{28,32},{36,40},{44,48},{52,56},{60,64},{68,... | collective-permute-start | bytes 73736 | tf_op jit(solution)/shard_map/ppermute | solution.py:504
  36.2 3.9 %collective-permute-done.refs_4_ = f32[48,128]{1,0:T(8,128)S(1)} collective-permute-done((f32[48,128]{1,0:T(8,128)S(1)}, f32[48,128]{1,0:T(8,128)S(1)}, u32[]{:S(2)}, u32[]{:S(2)}) %collective-permute-start) | collective-permute-done | bytes 24608 | tf_op jit(solution)/shard_map/ppermute | solution.py:504
  40.2 0.0 collective-permute-done.1.refs_3_
  40.2 0.0 collective-permute-done.2.refs_4_
  40.2 0.0 all-to-all-done
  40.2 0.0 collective-permute-done.3.refs_2_.refs_3_
  40.2 1.0 %take_rows.1 = f32[512,128]{1,0:T(8,128)} custom-call(f32[576,128]{1,0:T(8,128)S(1)} %bitcast.38, f32[128,128]{1,0:T(8,128)S(1)} %get-tuple-element.49.refs_1_.refs_0_, f32[152,128]{1,0:T(8,128)S(1)} %collective-permute-done.3.refs_2_.refs_3_), custom_call_target="tpu_custom_call" | custom-call | flops 2000000 | bytes 1000000 | tf_op jit(solution)/shard_map/take_rows/pallas_call | solution.py:509
  41.2 0.0 copy-start.2
  41.2 14.7 %all-to-all-start.1 = ((f32[64,8,128]{2,1,0:T(8,128)}), f32[64,8,128]{2,1,0:T(8,128)S(1)}, u32[]{:S(2)}, u32[]{:S(2)}) async-start(f32[64,8,128]{2,1,0:T(8,128)} %bitcast.20), calls=%async_computation.1 | async-start | bytes 524288 | tf_op jit(solution)/shard_map/all_to_all | solution.py:437
  55.9 0.0 copy-start
  55.9 0.0 copy-start.1
  56.0 0.3 reaction.1
  56.3 0.0 copy-start.8
  56.3 3.3 %collective-permute-start.4 = (f32[128,128]{1,0:T(8,128)S(1)}, f32[128,128]{1,0:T(8,128)S(1)}, u32[]{:S(2)}, u32[]{:S(2)}) collective-permute-start(f32[128,128]{1,0:T(8,128)S(1)} %get-tuple-element.56), channel_id=1, source_target_pairs={{0,4},{4,0},{8,12},{12,8},{16,20},{20,16},{24,28},{28,24},{32,36},... | collective-permute-start | bytes 196616 | tf_op jit(solution)/shard_map/ppermute | solution.py:443
  59.6 0.0 copy-done.2
  59.6 0.0 copy-done
  59.6 0.0 copy-done.1
  59.6 0.0 copy-done.8
  59.6 0.3 fine_own.1
  59.9 2.6 %bond_force.1.refs_1_ = f32[128,128]{1,0:T(8,128)S(1)} custom-call(f32[128,128]{1,0:T(8,128)S(1)} %get-tuple-element.49.refs_1_.refs_0_, s32[64,128]{1,0:T(8,128)S(1)} %bitcast.52, s32[64,128]{1,0:T(8,128)S(1)} %bitcast.56, f32[152,128]{1,0:T(8,128)S(1)} %collective-permute-done.3.refs_2_.refs_3_, f32[48,128]{1,0:T(8,128)S(1)} %collective-permute-done.refs_4_), custom_call_target="tpu_custom_call" | custom-call | flops 1000000000 | bytes 10000000 | tf_op jit(solution)/shard_map/bond_force/pallas_call | solution.py:523
  62.6 0.0 collective-permute-done.4.refs_6_
  62.6 0.7 %coarse_out.1 = (f32[128,128]{1,0:T(8,128)}, f32[128,128]{1,0:T(8,128)}) custom-call(f32[128,128]{1,0:T(8,128)S(1)} %get-tuple-element.49.refs_1_.refs_0_, f32[128,128]{1,0:T(8,128)S(1)} %bond_force.1.refs_1_, s32[64,128]{1,0:T(8,128)S(1)} %bitcast.53, f32[96,128]{1,0:T(8,128)S(1)} %collective-permute-done.1.refs_3_, ...), custom_call_target="tpu_custom_call" | custom-call | flops 10000000 | bytes 1000000 | tf_op jit(solution)/shard_map/coarse_out/pallas_call | solution.py:545
  63.3 4.1 %all-to-all-done.1 = f32[64,8,128]{2,1,0:T(8,128)S(1)} async-done(((f32[64,8,128]{2,1,0:T(8,128)}), f32[64,8,128]{2,1,0:T(8,128)S(1)}, u32[]{:S(2)}, u32[]{:S(2)}) %all-to-all-start.1) | async-done | bytes 262176 | tf_op jit(solution)/shard_map/all_to_all | solution.py:437
  67.4 1.1 %finish.1 = (f32[384,128]{1,0:T(8,128)}, f32[384,128]{1,0:T(8,128)}) custom-call(f32[512,128]{1,0:T(8,128)S(1)} %bitcast.40, f32[384,128]{1,0:T(8,128)S(1)} %get-tuple-element.64.refs_1_, f32[384,128]{1,0:T(8,128)S(1)} %get-tuple-element.65.refs_2_, bf16[96,256]{1,0:T(8,128)(2,1)S(1)} %get-tuple-element.66.refs_3_, ...), custom_call_target="tpu_custom_call" | custom-call | flops 1000000 | bytes 1000000 | tf_op jit(solution)/shard_map/finish/pallas_call | solution.py:564
  (1 shorter events, 0.0 us)
Async XLA Ops:
  3.0 23.1 %copy-start.3 = (f32[2,2,32,128]{3,2,1,0:T(8,128)S(1)}, f32[2,2,32,128]{3,2,1,0:T(8,128)}, u32[]{:S(2)}) copy-start(f32[2,2,32,128]{3,2,1,0:T(8,128)} %param.11) | copy-start | bytes 196612
  3.0 23.1 %copy-start.4 = (f32[2,2,32,128]{3,2,1,0:T(8,128)S(1)}, f32[2,2,32,128]{3,2,1,0:T(8,128)}, u32[]{:S(2)}) copy-start(f32[2,2,32,128]{3,2,1,0:T(8,128)} %param.12) | copy-start | bytes 196612
  3.0 23.1 %copy-start.5 = (s32[2,32,128]{2,1,0:T(8,128)S(1)}, s32[2,32,128]{2,1,0:T(8,128)}, u32[]{:S(2)}) copy-start(s32[2,32,128]{2,1,0:T(8,128)} %param.13) | copy-start | bytes 98308
  3.0 23.1 %copy-start.6 = (f32[2,2,32,128]{3,2,1,0:T(8,128)S(1)}, f32[2,2,32,128]{3,2,1,0:T(8,128)}, u32[]{:S(2)}) copy-start(f32[2,2,32,128]{3,2,1,0:T(8,128)} %param.10) | copy-start | bytes 196612
  3.0 23.1 %copy-start.7 = (s32[2,32,128]{2,1,0:T(8,128)S(1)}, s32[2,32,128]{2,1,0:T(8,128)}, u32[]{:S(2)}) copy-start(s32[2,32,128]{2,1,0:T(8,128)} %param.14) | copy-start | bytes 98308
  3.1 37.1 %all-to-all-start = ((f32[64,1,1152]{2,1,0:T(1,128)}), f32[64,1,1152]{2,1,0:T(1,128)S(1)}, u32[]{:S(2)}, u32[]{:S(2)}) async-start(f32[64,1,1152]{2,1,0:T(1,128)} %bitcast.16), calls=%async_computation | async-start | bytes 589824 | tf_op jit(solution)/shard_map/all_to_all | solution.py:437
  26.2 14.0 %collective-permute-start.3 = (f32[152,128]{1,0:T(8,128)S(1)}, f32[152,128]{1,0:T(8,128)S(1)}, u32[]{:S(2)}, u32[]{:S(2)}) collective-permute-start(f32[152,128]{1,0:T(8,128)S(1)} %get-tuple-element.48), channel_id=1, source_target_pairs={{0,4},{4,0},{8,12},{12,8},{16,20},{20,16},{24,28},{28,24},{32,36},... | collective-permute-start | bytes 233480 | tf_op jit(solution)/shard_map/ppermute | solution.py:443
  29.4 10.8 %collective-permute-start.1 = (f32[96,128]{1,0:T(8,128)S(1)}, f32[96,128]{1,0:T(8,128)S(1)}, u32[]{:S(2)}, u32[]{:S(2)}) collective-permute-start(f32[96,128]{1,0:T(8,128)S(1)} %get-tuple-element.44), channel_id=1, source_target_pairs={{0,1},{1,2},{2,3},{4,5},{5,6},{6,7},{8,9},{9,10},{10,11},{12,13},{... | collective-permute-start | bytes 147464 | tf_op jit(solution)/shard_map/ppermute | solution.py:507
  32.6 7.6 %collective-permute-start.2 = (f32[96,128]{1,0:T(8,128)S(1)}, f32[96,128]{1,0:T(8,128)S(1)}, u32[]{:S(2)}, u32[]{:S(2)}) collective-permute-start(f32[96,128]{1,0:T(8,128)S(1)} %get-tuple-element.45), channel_id=1, source_target_pairs={{1,0},{2,1},{3,2},{5,4},{6,5},{7,6},{9,8},{10,9},{11,10},{13,12},{... | collective-permute-start | bytes 147464 | tf_op jit(solution)/shard_map/ppermute | solution.py:507
  33.9 6.3 %collective-permute-start = (f32[48,128]{1,0:T(8,128)S(1)}, f32[48,128]{1,0:T(8,128)S(1)}, u32[]{:S(2)}, u32[]{:S(2)}) collective-permute-start(f32[48,128]{1,0:T(8,128)S(1)} %get-tuple-element.43), channel_id=1, source_target_pairs={{4,8},{12,16},{20,24},{28,32},{36,40},{44,48},{52,56},{60,64},{68,... | collective-permute-start | bytes 73736 | tf_op jit(solution)/shard_map/ppermute | solution.py:504
  41.2 18.4 %copy-start.2 = (f32[96,2,256]{2,1,0:T(2,128)S(1)}, f32[96,2,256]{2,1,0:T(2,128)}, u32[]{:S(2)}) copy-start(f32[96,2,256]{2,1,0:T(2,128)} %param.17) | copy-start | bytes 589828
  41.2 26.2 %all-to-all-start.1 = ((f32[64,8,128]{2,1,0:T(8,128)}), f32[64,8,128]{2,1,0:T(8,128)S(1)}, u32[]{:S(2)}, u32[]{:S(2)}) async-start(f32[64,8,128]{2,1,0:T(8,128)} %bitcast.20), calls=%async_computation.1 | async-start | bytes 524288 | tf_op jit(solution)/shard_map/all_to_all | solution.py:437
  55.9 3.7 %copy-start = (f32[96,2,256]{2,1,0:T(2,128)S(1)}, f32[96,2,256]{2,1,0:T(2,128)}, u32[]{:S(2)}) copy-start(f32[96,2,256]{2,1,0:T(2,128)} %param.15) | copy-start | bytes 589828
  55.9 3.7 %copy-start.1 = (f32[96,2,256]{2,1,0:T(2,128)S(1)}, f32[96,2,256]{2,1,0:T(2,128)}, u32[]{:S(2)}) copy-start(f32[96,2,256]{2,1,0:T(2,128)} %param.16) | copy-start | bytes 589828
  56.3 3.3 %copy-start.8 = (s32[96,1]{0,1:T(1,128)S(1)}, s32[96,1]{0,1:T(1,128)}, u32[]{:S(2)}) copy-start(s32[96,1]{0,1:T(1,128)} %param.18) | copy-start | bytes 1156
  56.3 6.3 %collective-permute-start.4 = (f32[128,128]{1,0:T(8,128)S(1)}, f32[128,128]{1,0:T(8,128)S(1)}, u32[]{:S(2)}, u32[]{:S(2)}) collective-permute-start(f32[128,128]{1,0:T(8,128)S(1)} %get-tuple-element.56), channel_id=1, source_target_pairs={{0,4},{4,0},{8,12},{12,8},{16,20},{20,16},{24,28},{28,24},{32,36},... | collective-permute-start | bytes 196616 | tf_op jit(solution)/shard_map/ppermute | solution.py:443

commit v4 on v3

--- a/solution.py
+++ b/solution.py
@@ -16,17 +16,18 @@
     return lax.broadcasted_iota(I32, shape, dim)
 
 
-def place(chip, chips):
+def place(chip, chips, core):
     if chips != 64:
         return chip
-    return chip ^ 40
+    lead = 9 - 1 * core
+    return ((chip & 48) ^ 32) | ((chip - lead) & 15)
 
 
 def slot_of(owner, rank, patches):
     chips = patches // 2
     core = lax.axis_index("patch") & 1
     group = ((owner & 1) ^ core) * 2 + rank
-    return group * chips + place(owner >> 1, chips)
+    return group * chips + place(owner >> 1, chips, core)
 
 
 def split3(x):
@@ -432,8 +433,10 @@
 
 def exchange(x, patches):
     chips = patches // 2
-    order = sorted(range(chips), key=lambda chip: place(chip, chips))
-    groups = [[2 * chip + core for chip in order] for core in range(2)]
+    groups = [
+        [2 * chip + core for chip in sorted(range(chips), key=lambda x: place(x, chips, core))]
+        for core in range(2)
+    ]
     return lax.all_to_all(
         x, "patch", split_axis=0, concat_axis=0, tiled=True, axis_index_groups=groups
     )

time: 68.9 us -> 68.7 us (level)
    ppermute x2, starting transfers between devices: 6.42 us -> 5.37 us  [to_other_core(): return lax.ppermute(x, 'patch', [(i, i ^ 1) for i in range(patches)])]
    ppermute x1, starting transfers between devices: 2.38 us -> 3.28 us  [body(): edge = lax.ppermute(edge, 'patch', pairs + [(b, a) for a, b in pairs])]
where the time goes in v4:
time: 68.7 us; the launch traced here: 68.1 us
  starting transfers between devices  50.9 us (74%)
  Pallas kernels  8.46 us (12%)
  waiting for transfers between devices  7.84 us (11%)
  between operations  0.88 us (1%)
    all_to_all x2, starting transfers between devices, exchange(): lax.all_to_all(x, 'patch', split_axis=0, concat_axis=0, tiled=True, axis_...  37.8 us
    ppermute x2, starting transfers between devices, to_other_core(): return lax.ppermute(x, 'patch', [(i, i ^ 1) for i in range(patches)])  5.37 us
    all_to_all x2, waiting for transfers between devices, exchange(): lax.all_to_all(x, 'patch', split_axis=0, concat_axis=0, tiled=True, axis_...  3.97 us
    ppermute x1, waiting for transfers between devices, body(): edge = lax.ppermute(edge, 'patch', pairs + [(b, a) for a, b in pairs])  3.86 us
    ppermute x1, starting transfers between devices, body(): edge = lax.ppermute(edge, 'patch', pairs + [(b, a) for a, b in pairs])  3.28 us
    ppermute x1, starting transfers between devices, body(): lax.ppermute(below, 'slab', up)  3.2 us
    pallas_call x1, Pallas kernels, body(): call(lambda *refs: bond_kernel(inner_x, *refs), shape(2 * rows, cells), '...  2.65 us
    pallas_call x1, Pallas kernels, body(): call(lambda *refs: pack_kernel(blocks, patches, cells, *refs), shape(OUT_...  2.36 us
  transfers between devices with their start and end apart: 7, of which 2 were waited for; matrix products, arithmetic and copies ran while one was open for 0% of the time, Pallas kernels for 6%

profile of v4, /device:TPU:1, one launch (start us, length us, event | category | flops | bytes accessed | tf_op | source)
XLA Modules:
  0.0 68.1 jit_solution(14242956995059791617)
XLA Ops:
  0.6 2.4 %pack_fine.1 = f32[576,128]{1,0:T(8,128)} custom-call(s32[1,96]{1,0:T(1,128)} %bitcast.57, s32[1,96]{1,0:T(1,128)} %bitcast.59, f32[384,128]{1,0:T(8,128)} %bitcast.41, f32[384,128]{1,0:T(8,128)} %bitcast.43, f32[384,128]{1,0:T(8,128)} %bitcast.45), custom_call_target="tpu_custom_call" | custom-call | flops 2000000 | bytes 1000000 | tf_op jit(solution)/shard_map/pack_fine/pallas_call | solution.py:474
  3.0 0.0 copy-start.3
  3.0 0.0 copy-start.4
  3.0 0.0 copy-start.5
  3.0 0.0 copy-start.6
  3.0 0.0 copy-start.7
  3.1 23.1 %all-to-all-start = ((f32[64,1,1152]{2,1,0:T(1,128)}), f32[64,1,1152]{2,1,0:T(1,128)S(1)}, u32[]{:S(2)}, u32[]{:S(2)}) async-start(f32[64,1,1152]{2,1,0:T(1,128)} %bitcast.16), calls=%async_computation | async-start | bytes 589824 | tf_op jit(solution)/shard_map/all_to_all | solution.py:440
  26.1 0.0 copy-done.3
  26.1 0.0 copy-done.4
  26.1 0.0 copy-done.5
  26.1 0.0 copy-done.6
  26.2 0.0 copy-done.7
  26.2 2.2 %collective-permute-start.3 = (f32[152,128]{1,0:T(8,128)S(1)}, f32[152,128]{1,0:T(8,128)S(1)}, u32[]{:S(2)}, u32[]{:S(2)}) collective-permute-start(f32[152,128]{1,0:T(8,128)S(1)} %get-tuple-element.48), channel_id=1, source_target_pairs={{0,4},{4,0},{8,12},{12,8},{16,20},{20,16},{24,28},{28,24},{32,36},... | collective-permute-start | bytes 233480 | tf_op jit(solution)/shard_map/ppermute | solution.py:446
  28.4 3.2 %collective-permute-start.1 = (f32[96,128]{1,0:T(8,128)S(1)}, f32[96,128]{1,0:T(8,128)S(1)}, u32[]{:S(2)}, u32[]{:S(2)}) collective-permute-start(f32[96,128]{1,0:T(8,128)S(1)} %get-tuple-element.44), channel_id=1, source_target_pairs={{0,1},{1,2},{2,3},{4,5},{5,6},{6,7},{8,9},{9,10},{10,11},{12,13},{... | collective-permute-start | bytes 147464 | tf_op jit(solution)/shard_map/ppermute | solution.py:510
  31.7 1.3 %collective-permute-start.2 = (f32[96,128]{1,0:T(8,128)S(1)}, f32[96,128]{1,0:T(8,128)S(1)}, u32[]{:S(2)}, u32[]{:S(2)}) collective-permute-start(f32[96,128]{1,0:T(8,128)S(1)} %get-tuple-element.45), channel_id=1, source_target_pairs={{1,0},{2,1},{3,2},{5,4},{6,5},{7,6},{9,8},{10,9},{11,10},{13,12},{... | collective-permute-start | bytes 147464 | tf_op jit(solution)/shard_map/ppermute | solution.py:510
  33.0 3.3 %collective-permute-start = (f32[48,128]{1,0:T(8,128)S(1)}, f32[48,128]{1,0:T(8,128)S(1)}, u32[]{:S(2)}, u32[]{:S(2)}) collective-permute-start(f32[48,128]{1,0:T(8,128)S(1)} %get-tuple-element.43), channel_id=1, source_target_pairs={{4,8},{12,16},{20,24},{28,32},{36,40},{44,48},{52,56},{60,64},{68,... | collective-permute-start | bytes 73736 | tf_op jit(solution)/shard_map/ppermute | solution.py:507
  36.2 3.9 %collective-permute-done.refs_4_ = f32[48,128]{1,0:T(8,128)S(1)} collective-permute-done((f32[48,128]{1,0:T(8,128)S(1)}, f32[48,128]{1,0:T(8,128)S(1)}, u32[]{:S(2)}, u32[]{:S(2)}) %collective-permute-start) | collective-permute-done | bytes 24608 | tf_op jit(solution)/shard_map/ppermute | solution.py:507
  40.1 0.0 collective-permute-done.1.refs_3_
  40.1 0.0 collective-permute-done.2.refs_4_
  40.1 0.0 all-to-all-done
  40.1 0.0 collective-permute-done.3.refs_2_.refs_3_
  40.1 1.0 %take_rows.1 = f32[512,128]{1,0:T(8,128)} custom-call(f32[576,128]{1,0:T(8,128)S(1)} %bitcast.38, f32[128,128]{1,0:T(8,128)S(1)} %get-tuple-element.49.refs_1_.refs_0_, f32[152,128]{1,0:T(8,128)S(1)} %collective-permute-done.3.refs_2_.refs_3_), custom_call_target="tpu_custom_call" | custom-call | flops 2000000 | bytes 1000000 | tf_op jit(solution)/shard_map/take_rows/pallas_call | solution.py:512
  41.1 0.0 copy-start.2
  41.1 14.7 %all-to-all-start.1 = ((f32[64,8,128]{2,1,0:T(8,128)}), f32[64,8,128]{2,1,0:T(8,128)S(1)}, u32[]{:S(2)}, u32[]{:S(2)}) async-start(f32[64,8,128]{2,1,0:T(8,128)} %bitcast.20), calls=%async_computation.1 | async-start | bytes 524288 | tf_op jit(solution)/shard_map/all_to_all | solution.py:440
  55.8 0.0 copy-start
  55.9 0.0 copy-start.1
  55.9 0.3 reaction.1
  56.2 0.0 copy-start.8
  56.2 3.1 %collective-permute-start.4 = (f32[128,128]{1,0:T(8,128)S(1)}, f32[128,128]{1,0:T(8,128)S(1)}, u32[]{:S(2)}, u32[]{:S(2)}) collective-permute-start(f32[128,128]{1,0:T(8,128)S(1)} %get-tuple-element.56), channel_id=1, source_target_pairs={{0,4},{4,0},{8,12},{12,8},{16,20},{20,16},{24,28},{28,24},{32,36},... | collective-permute-start | bytes 196616 | tf_op jit(solution)/shard_map/ppermute | solution.py:446
  59.4 0.0 copy-done.2
  59.4 0.0 copy-done
  59.4 0.0 copy-done.1
  59.4 0.0 copy-done.8
  59.4 0.3 fine_own.1
  59.7 2.6 %bond_force.1.refs_1_ = f32[128,128]{1,0:T(8,128)S(1)} custom-call(f32[128,128]{1,0:T(8,128)S(1)} %get-tuple-element.49.refs_1_.refs_0_, s32[64,128]{1,0:T(8,128)S(1)} %bitcast.52, s32[64,128]{1,0:T(8,128)S(1)} %bitcast.56, f32[152,128]{1,0:T(8,128)S(1)} %collective-permute-done.3.refs_2_.refs_3_, f32[48,128]{1,0:T(8,128)S(1)} %collective-permute-done.refs_4_), custom_call_target="tpu_custom_call" | custom-call | flops 1000000000 | bytes 10000000 | tf_op jit(solution)/shard_map/bond_force/pallas_call | solution.py:526
  62.4 0.0 collective-permute-done.4.refs_6_
  62.4 0.7 %coarse_out.1 = (f32[128,128]{1,0:T(8,128)}, f32[128,128]{1,0:T(8,128)}) custom-call(f32[128,128]{1,0:T(8,128)S(1)} %get-tuple-element.49.refs_1_.refs_0_, f32[128,128]{1,0:T(8,128)S(1)} %bond_force.1.refs_1_, s32[64,128]{1,0:T(8,128)S(1)} %bitcast.53, f32[96,128]{1,0:T(8,128)S(1)} %collective-permute-done.1.refs_3_, ...), custom_call_target="tpu_custom_call" | custom-call | flops 10000000 | bytes 1000000 | tf_op jit(solution)/shard_map/coarse_out/pallas_call | solution.py:548
  63.1 4.0 %all-to-all-done.1 = f32[64,8,128]{2,1,0:T(8,128)S(1)} async-done(((f32[64,8,128]{2,1,0:T(8,128)}), f32[64,8,128]{2,1,0:T(8,128)S(1)}, u32[]{:S(2)}, u32[]{:S(2)}) %all-to-all-start.1) | async-done | bytes 262176 | tf_op jit(solution)/shard_map/all_to_all | solution.py:440
  67.0 1.1 %finish.1 = (f32[384,128]{1,0:T(8,128)}, f32[384,128]{1,0:T(8,128)}) custom-call(f32[512,128]{1,0:T(8,128)S(1)} %bitcast.40, f32[384,128]{1,0:T(8,128)S(1)} %get-tuple-element.64.refs_1_, f32[384,128]{1,0:T(8,128)S(1)} %get-tuple-element.65.refs_2_, bf16[96,256]{1,0:T(8,128)(2,1)S(1)} %get-tuple-element.66.refs_3_, ...), custom_call_target="tpu_custom_call" | custom-call | flops 1000000 | bytes 1000000 | tf_op jit(solution)/shard_map/finish/pallas_call | solution.py:567
  (1 shorter events, 0.0 us)
Async XLA Ops:
  3.0 23.1 %copy-start.3 = (f32[2,2,32,128]{3,2,1,0:T(8,128)S(1)}, f32[2,2,32,128]{3,2,1,0:T(8,128)}, u32[]{:S(2)}) copy-start(f32[2,2,32,128]{3,2,1,0:T(8,128)} %param.11) | copy-start | bytes 196612
  3.0 23.1 %copy-start.4 = (f32[2,2,32,128]{3,2,1,0:T(8,128)S(1)}, f32[2,2,32,128]{3,2,1,0:T(8,128)}, u32[]{:S(2)}) copy-start(f32[2,2,32,128]{3,2,1,0:T(8,128)} %param.12) | copy-start | bytes 196612
  3.0 23.1 %copy-start.5 = (s32[2,32,128]{2,1,0:T(8,128)S(1)}, s32[2,32,128]{2,1,0:T(8,128)}, u32[]{:S(2)}) copy-start(s32[2,32,128]{2,1,0:T(8,128)} %param.13) | copy-start | bytes 98308
  3.0 23.1 %copy-start.6 = (f32[2,2,32,128]{3,2,1,0:T(8,128)S(1)}, f32[2,2,32,128]{3,2,1,0:T(8,128)}, u32[]{:S(2)}) copy-start(f32[2,2,32,128]{3,2,1,0:T(8,128)} %param.10) | copy-start | bytes 196612
  3.0 23.1 %copy-start.7 = (s32[2,32,128]{2,1,0:T(8,128)S(1)}, s32[2,32,128]{2,1,0:T(8,128)}, u32[]{:S(2)}) copy-start(s32[2,32,128]{2,1,0:T(8,128)} %param.14) | copy-start | bytes 98308
  3.1 37.1 %all-to-all-start = ((f32[64,1,1152]{2,1,0:T(1,128)}), f32[64,1,1152]{2,1,0:T(1,128)S(1)}, u32[]{:S(2)}, u32[]{:S(2)}) async-start(f32[64,1,1152]{2,1,0:T(1,128)} %bitcast.16), calls=%async_computation | async-start | bytes 589824 | tf_op jit(solution)/shard_map/all_to_all | solution.py:440
  26.2 13.9 %collective-permute-start.3 = (f32[152,128]{1,0:T(8,128)S(1)}, f32[152,128]{1,0:T(8,128)S(1)}, u32[]{:S(2)}, u32[]{:S(2)}) collective-permute-start(f32[152,128]{1,0:T(8,128)S(1)} %get-tuple-element.48), channel_id=1, source_target_pairs={{0,4},{4,0},{8,12},{12,8},{16,20},{20,16},{24,28},{28,24},{32,36},... | collective-permute-start | bytes 233480 | tf_op jit(solution)/shard_map/ppermute | solution.py:446
  28.4 11.7 %collective-permute-start.1 = (f32[96,128]{1,0:T(8,128)S(1)}, f32[96,128]{1,0:T(8,128)S(1)}, u32[]{:S(2)}, u32[]{:S(2)}) collective-permute-start(f32[96,128]{1,0:T(8,128)S(1)} %get-tuple-element.44), channel_id=1, source_target_pairs={{0,1},{1,2},{2,3},{4,5},{5,6},{6,7},{8,9},{9,10},{10,11},{12,13},{... | collective-permute-start | bytes 147464 | tf_op jit(solution)/shard_map/ppermute | solution.py:510
  31.7 8.5 %collective-permute-start.2 = (f32[96,128]{1,0:T(8,128)S(1)}, f32[96,128]{1,0:T(8,128)S(1)}, u32[]{:S(2)}, u32[]{:S(2)}) collective-permute-start(f32[96,128]{1,0:T(8,128)S(1)} %get-tuple-element.45), channel_id=1, source_target_pairs={{1,0},{2,1},{3,2},{5,4},{6,5},{7,6},{9,8},{10,9},{11,10},{13,12},{... | collective-permute-start | bytes 147464 | tf_op jit(solution)/shard_map/ppermute | solution.py:510
  33.0 7.1 %collective-permute-start = (f32[48,128]{1,0:T(8,128)S(1)}, f32[48,128]{1,0:T(8,128)S(1)}, u32[]{:S(2)}, u32[]{:S(2)}) collective-permute-start(f32[48,128]{1,0:T(8,128)S(1)} %get-tuple-element.43), channel_id=1, source_target_pairs={{4,8},{12,16},{20,24},{28,32},{36,40},{44,48},{52,56},{60,64},{68,... | collective-permute-start | bytes 73736 | tf_op jit(solution)/shard_map/ppermute | solution.py:507
  41.1 18.2 %copy-start.2 = (f32[96,2,256]{2,1,0:T(2,128)S(1)}, f32[96,2,256]{2,1,0:T(2,128)}, u32[]{:S(2)}) copy-start(f32[96,2,256]{2,1,0:T(2,128)} %param.17) | copy-start | bytes 589828
  41.1 25.9 %all-to-all-start.1 = ((f32[64,8,128]{2,1,0:T(8,128)}), f32[64,8,128]{2,1,0:T(8,128)S(1)}, u32[]{:S(2)}, u32[]{:S(2)}) async-start(f32[64,8,128]{2,1,0:T(8,128)} %bitcast.20), calls=%async_computation.1 | async-start | bytes 524288 | tf_op jit(solution)/shard_map/all_to_all | solution.py:440
  55.8 3.5 %copy-start = (f32[96,2,256]{2,1,0:T(2,128)S(1)}, f32[96,2,256]{2,1,0:T(2,128)}, u32[]{:S(2)}) copy-start(f32[96,2,256]{2,1,0:T(2,128)} %param.15) | copy-start | bytes 589828
  55.9 3.5 %copy-start.1 = (f32[96,2,256]{2,1,0:T(2,128)S(1)}, f32[96,2,256]{2,1,0:T(2,128)}, u32[]{:S(2)}) copy-start(f32[96,2,256]{2,1,0:T(2,128)} %param.16) | copy-start | bytes 589828
  56.2 3.2 %copy-start.8 = (s32[96,1]{0,1:T(1,128)S(1)}, s32[96,1]{0,1:T(1,128)}, u32[]{:S(2)}) copy-start(s32[96,1]{0,1:T(1,128)} %param.18) | copy-start | bytes 1156
  56.2 6.1 %collective-permute-start.4 = (f32[128,128]{1,0:T(8,128)S(1)}, f32[128,128]{1,0:T(8,128)S(1)}, u32[]{:S(2)}, u32[]{:S(2)}) collective-permute-start(f32[128,128]{1,0:T(8,128)S(1)} %get-tuple-element.56), channel_id=1, source_target_pairs={{0,4},{4,0},{8,12},{12,8},{16,20},{20,16},{24,28},{28,24},{32,36},... | collective-permute-start | bytes 196616 | tf_op jit(solution)/shard_map/ppermute | solution.py:446
